TPU v7x, 256 devices: a whole 4x4x8 slice. The times are simulated.
256 devices in a mesh: seq: 32 (over z, y), cache: 4 (over x), mp: 2 (over core).
Axes of the slice: x: 4, y: 4, z: 8, core: 2. Of those that a mesh axis runs over, the one named last changes fastest.
Arguments:
- tokens: bfloat16 [12288, 3072], P('seq'), as said below
- query_weight: bfloat16 [3072, 2048], P(None, ('cache', 'mp')), as said below
- key_weight: bfloat16 [3072, 2048], P(None, ('cache', 'mp')), as said below
- value_weight: bfloat16 [3072, 2048], P(None, ('cache', 'mp')), may hold values from -0.109375 to 0.109375
- output_weight: bfloat16 [2048, 3072], P(('cache', 'mp')), may hold values from -1.5 to 1.5
- adapter_down_maps: bfloat16 [8, 3072, 128], P('cache'), may hold values from -0.109375 to 0.109375
- adapter_up_maps: bfloat16 [8, 2, 64, 2048], P('cache'), may hold values from -0.75 to 0.75
- request_lengths: int32 [16], replicated, may hold values from 1 to 6528, 12288 in all
- request_adapter: int32 [16], replicated, may hold values from 0 to 7
- adapter_slot: int32 [8], replicated, may hold values from 0 to 7, each once
Outputs:
- attn_out: bfloat16 [12288, 3072], P('seq', ('cache', 'mp'))
Inputs may be any that keep to these rules, and one draw needn't show every extreme that they name: `tokens`: values of order one. `query_weight`: entries of order 1 / sqrt(3072). `key_weight`: entries of order 1 / sqrt(3072). `request_lengths`: the 16 lengths sum to 12288; the longest is exactly 6528. `adapter_slot`: each slot holds exactly one adapter.
All inputs are finite; a program needn't handle non-finite values.
Results may differ from a plain program's by a relative error of at most 0.02.
Values may be sent and summed in bfloat16 or wider, within the bound.
No kernel may reach another device: no remote copies, remote signals or barrier semaphores. Data moves between devices by JAX's collectives and lax.ppermute only.
A program may use at most 128 MiB of HBM per device.

v0:
```python
import functools
import itertools
import math

import jax
import jax.numpy as jnp
from jax import lax
from jax.experimental import pallas as pl
from jax.experimental.pallas import tpu as pltpu
from jax.sharding import PartitionSpec as P

HEAD = 128
SEQ_Z = 8
SEQ_Y = 4
CACHE = 4
REQUESTS = 16
PLACES = 3
START = -1e30
NEG = -3e30
TAIL = 16
QUERY_SCALE = HEAD ** (-0.5) * math.log2(math.e)


CHUNKS = 6
ATTEND_FLOPS = 10**9


def around_z(step):
    return [
        (z * SEQ_Y + y, (z + step) % SEQ_Z * SEQ_Y + y) for z in range(SEQ_Z) for y in range(SEQ_Y)
    ]


def around_y(step):
    return [
        (z * SEQ_Y + y, z * SEQ_Y + (y + step) % SEQ_Y) for z in range(SEQ_Z) for y in range(SEQ_Y)
    ]


def around_x(step):
    return [(x, (x + step) % CACHE) for x in range(CACHE)]


def matmul(a, b, dims=((1,), (0,))):
    return lax.dot_general(a, b, (dims, ((), ())), preferred_element_type=jnp.float32)


def whole(shape):
    return pl.BlockSpec(shape, lambda *at: (0,) * len(shape))


def request_ends(known):
    bounds, at = [], jnp.int32(0)
    for r in range(REQUESTS):
        bounds.append((at, at + known[PLACES + r]))
        at = at + known[PLACES + r]
    return bounds


def slots_of_rows(places, known):
    found = jnp.zeros(places.shape, jnp.int32)
    for r, (start, _) in enumerate(request_ends(known)):
        found = jnp.where(places >= start, known[PLACES + 2 * REQUESTS + known[PLACES + REQUESTS + r]], found)
    return found


def lower_kernel(where, tokens, down, ups, *refs):
    outs, (held, maps, columns, arrived) = refs[:CACHE], refs[CACHE:]
    row_total, width = tokens.shape
    slot_total, _, low = down.shape
    up_rows = ups.shape[0]
    col_count = columns.shape[2]
    deep = width // CHUNKS
    copies = []
    for chunk in range(CHUNKS):
        part = pl.ds(chunk * deep, deep)
        copies.append(
            [pltpu.make_async_copy(tokens.at[:, part], held.at[chunk], arrived.at[chunk * 4])]
            + [
                pltpu.make_async_copy(down.at[slot, part], maps.at[chunk, slot], arrived.at[chunk * 4 + 1 + slot])
                for slot in range(slot_total)
            ]
        )
    for chunk in range(CHUNKS):
        for copy in copies[chunk]:
            copy.start()
    up_copies = []
    for step in range(CACHE):
        first = pl.multiple_of((lax.rem(where[1] + step, CACHE) * 2 + where[2]) * col_count, HEAD)
        up_copies.append(
            pltpu.make_async_copy(ups.at[:, pl.ds(first, col_count)], columns.at[step], arrived.at[CHUNKS * 4 + step])
        )
        up_copies[-1].start()
    places = where[0] * row_total + lax.broadcasted_iota(jnp.int32, (row_total, low), 0)
    mine = slots_of_rows(places, where)
    total = None
    for chunk in range(CHUNKS):
        for copy in copies[chunk]:
            copy.wait()
        pair = jnp.concatenate([maps[chunk, slot] for slot in range(slot_total)], axis=1)
        product = matmul(held[chunk], pair)
        total = product if total is None else total + product
    rows = jnp.zeros((row_total, low), jnp.float32)
    for slot in range(slot_total):
        rows = jnp.where(
            mine == where[1] * slot_total + slot, total[:, slot * low : (slot + 1) * low], rows
        )
    rows = rows.astype(jnp.bfloat16)
    for step, out in enumerate(outs):
        up_copies[step].wait()
        out[0:row_total, :] = rows
        for half in range(col_count // HEAD):
            at = row_total + half * up_rows
            out[at : at + up_rows, :] = columns[step, :, half * HEAD : (half + 1) * HEAD]


def lower(where, tokens, down, ups, col_count):
    row_total, width = tokens.shape
    slot_total, _, low = down.shape
    up_rows = ups.shape[0]
    deep = width // CHUNKS
    out_rows = row_total + up_rows * col_count // HEAD
    return pl.pallas_call(
        lower_kernel,
        grid_spec=pltpu.PrefetchScalarGridSpec(
            num_scalar_prefetch=1,
            grid=(1,),
            in_specs=[pl.BlockSpec(memory_space=pltpu.HBM)] * 3,
            out_specs=[whole((out_rows, HEAD))] * CACHE,
            scratch_shapes=[
                pltpu.VMEM((CHUNKS, row_total, deep), jnp.bfloat16),
                pltpu.VMEM((CHUNKS, slot_total, deep, low), jnp.bfloat16),
                pltpu.VMEM((CACHE, up_rows, col_count), jnp.bfloat16),
                pltpu.SemaphoreType.DMA((CHUNKS * 4 + CACHE,)),
            ],
        ),
        out_shape=[jax.ShapeDtypeStruct((out_rows, HEAD), jnp.bfloat16)] * CACHE,
        compiler_params=pltpu.CompilerParams(vmem_limit_bytes=62 * 2**20),
        cost_estimate=pl.CostEstimate(flops=6 * 10**8, bytes_accessed=6 * 2**20, transcendentals=0),
    )(where, tokens, down, ups)


def query_kernel(steps, where, tokens, wq, query, spans, info, total):
    step = pl.program_id(0)
    row_total = tokens.shape[0]
    held = tokens[...]

    @pl.when(step == 0)
    def _():
        total[...] = matmul(held, wq[...])
        bounds = request_ends(where)
        seq = where[0]
        seq_z, seq_y = lax.div(seq, SEQ_Y), lax.rem(seq, SEQ_Y)

        def request_at(row):
            found = jnp.int32(0)
            for _, end in bounds:
                found = found + (row >= end).astype(jnp.int32)
            return found

        def groups_row(group):
            return (seq_z * SEQ_Y + lax.rem(seq_y + SEQ_Y - group, SEQ_Y)) * row_total

        for group in range(SEQ_Y):
            row = groups_row(group)
            info[2 * group] = request_at(row)
            info[2 * group + 1] = request_at(row + row_total - 1)
            places = row + lax.broadcasted_iota(jnp.int32, (8, row_total), 1)
            starts = jnp.zeros(places.shape, jnp.int32)
            ends = jnp.zeros(places.shape, jnp.int32)
            for start, end in bounds:
                starts = jnp.where(places >= start, start, starts)
                ends = jnp.where(places >= start, end, ends)
            index = lax.broadcasted_iota(jnp.int32, (8, row_total), 0)
            cols = slice(group % 2 * row_total, group % 2 * row_total + row_total)
            spans[group // 2, :, cols] = jnp.where(index == 0, starts, ends)
        for back in range(SEQ_Z):
            row = (lax.rem(seq_z + SEQ_Z - back, SEQ_Z) * SEQ_Y + seq_y) * row_total
            info[8 + 3 * back] = request_at(row)
            info[8 + 3 * back + 1] = request_at(row + row_total - 1)
            info[8 + 3 * back + 2] = row

    @pl.when(step > 0)
    def _():
        total[...] += matmul(held, wq[...])

    @pl.when(step == steps - 1)
    def _():
        scaled = total[...] * QUERY_SCALE
        for head in range(query.shape[0]):
            query[head] = scaled[:, head * HEAD : (head + 1) * HEAD].T.astype(jnp.bfloat16)


def project_query(where, tokens, wq):
    steps = 3
    row_total, width = tokens.shape
    col_count = wq.shape[1]
    heads = col_count // HEAD
    deep = width // steps
    return pl.pallas_call(
        functools.partial(query_kernel, steps),
        grid_spec=pltpu.PrefetchScalarGridSpec(
            num_scalar_prefetch=1,
            grid=(steps,),
            in_specs=[
                pl.BlockSpec((row_total, deep), lambda i, *rest: (0, i)),
                pl.BlockSpec((deep, col_count), lambda i, *rest: (i, 0)),
            ],
            out_specs=[
                whole((heads, HEAD, row_total)),
                whole((SEQ_Y // 2, 8, 2 * row_total)),
                pl.BlockSpec(memory_space=pltpu.SMEM),
            ],
            scratch_shapes=[pltpu.VMEM((row_total, col_count), jnp.float32)],
        ),
        out_shape=[
            jax.ShapeDtypeStruct((heads, HEAD, row_total), jnp.bfloat16),
            jax.ShapeDtypeStruct((SEQ_Y // 2, 8, 2 * row_total), jnp.int32),
            jax.ShapeDtypeStruct((8 + 3 * SEQ_Z,), jnp.int32),
        ],
        compiler_params=pltpu.CompilerParams(vmem_limit_bytes=24 * 2**20),
        cost_estimate=pl.CostEstimate(flops=6 * 10**8, bytes_accessed=4 * 2**20, transcendentals=0),
    )(where, tokens, wq)


def project_kernel(tokens, wk, wv, key, value):
    held = tokens[...]

    @pl.when(pl.program_id(0) == 0)
    def _():
        key[...] = matmul(held, wk[...])
        value[...] = matmul(held, wv[...])

    @pl.when(pl.program_id(0) > 0)
    def _():
        key[...] += matmul(held, wk[...])
        value[...] += matmul(held, wv[...])


def project(tokens, wk, wv):
    steps = 3
    row_total, width = tokens.shape
    col_count = wk.shape[1]
    deep = width // steps
    weight = pl.BlockSpec((deep, col_count), lambda i: (i, 0))
    summed = jax.ShapeDtypeStruct((row_total, col_count), jnp.float32)
    return pl.pallas_call(
        project_kernel,
        grid=(steps,),
        in_specs=[pl.BlockSpec((row_total, deep), lambda i: (0, i)), weight, weight],
        out_specs=[whole((row_total, col_count))] * 2,
        out_shape=[summed, summed],
        compiler_params=pltpu.CompilerParams(vmem_limit_bytes=24 * 2**20),
        cost_estimate=pl.CostEstimate(flops=12 * 10**8, bytes_accessed=6 * 2**20, transcendentals=0),
    )(tokens, wk, wv)


def adapt_kernel(slot_total, where, key, value, *refs):
    messages, out = refs[:-1], refs[-1]
    row_total = key.shape[0]
    low = functools.reduce(jnp.add, [m[0:row_total, :].astype(jnp.float32) for m in messages])
    places = where[0] * row_total + lax.broadcasted_iota(jnp.int32, low.shape, 0)
    mine = slots_of_rows(places, where)
    for_key = lax.broadcasted_iota(jnp.int32, low.shape, 1) < low.shape[1] // 2
    key_low, value_low = [], []
    for step in range(len(messages)):
        for slot in range(slot_total):
            holder = lax.rem(where[1] + CACHE - step, CACHE) * slot_total + slot
            rows = jnp.where(mine == holder, low, 0.0)
            key_low.append(jnp.where(for_key, rows, 0.0).astype(jnp.bfloat16))
            value_low.append(jnp.where(for_key, 0.0, rows).astype(jnp.bfloat16))
    key_low, value_low = jnp.concatenate(key_low, axis=1), jnp.concatenate(value_low, axis=1)
    up_rows = slot_total * low.shape[1]
    for head in range(out.shape[0]):
        cols = slice(head * HEAD, (head + 1) * HEAD)
        at = row_total + head * up_rows
        up = jnp.concatenate([m[at : at + up_rows, :] for m in messages], axis=0)
        out[head, 0:row_total, :] = (key[:, cols] + matmul(key_low, up)).astype(jnp.bfloat16)
        summed = value[:, cols] + matmul(value_low, up)
        for part in range(row_total // HEAD):
            rows = slice(part * HEAD, (part + 1) * HEAD)
            out[head, row_total + part * HEAD : row_total + (part + 1) * HEAD, :] = summed[
                rows, :
            ].T.astype(jnp.bfloat16)


def adapt(where, key, value, messages, slot_total):
    row_total, col_count = key.shape
    heads = col_count // HEAD
    return pl.pallas_call(
        functools.partial(adapt_kernel, slot_total),
        grid_spec=pltpu.PrefetchScalarGridSpec(
            num_scalar_prefetch=1,
            grid=(1,),
            in_specs=[whole(a.shape) for a in (key, value, *messages)],
            out_specs=whole((heads, 2 * row_total, HEAD)),
        ),
        out_shape=jax.ShapeDtypeStruct((heads, 2 * row_total, HEAD), jnp.bfloat16),
        compiler_params=pltpu.CompilerParams(vmem_limit_bytes=32 * 2**20),
        cost_estimate=pl.CostEstimate(flops=4 * 10**8, bytes_accessed=2 * 2**20, transcendentals=0),
    )(where, key, value, *messages)


def attend_kernel(first, last, backs, info, queries, span, *refs):
    at = 0
    blocks = []
    for back in backs:
        width = 2 if back == SEQ_Z // 2 else 1
        blocks.append(refs[at : at + width])
        at += width
    if not first:
        state_in, sums_in = refs[at : at + 2]
        at += 2
    outs = refs[at:]
    state, sums = outs[-2:]
    outs = outs[:-2]
    pair, head = pl.program_id(0), pl.program_id(1)
    columns = queries.shape[1]
    row_total = columns // 2
    if first:
        state[...] = jnp.zeros(state.shape, jnp.float32)
        sums[0:1, :] = jnp.full((1, columns), START, jnp.float32)
        sums[1:2, :] = jnp.zeros((1, columns), jnp.float32)
    else:
        state[...] = state_in[...]
        sums[...] = sums_in[...]
    a_first, a_last = info[4 * pair], info[4 * pair + 1]
    b_first, b_last = info[4 * pair + 2], info[4 * pair + 3]
    index = lax.broadcasted_iota(jnp.int32, (TAIL, row_total), 0)
    ones = jnp.where(index == 0, 1.0, 0.0).astype(jnp.bfloat16)

    def meets(back):
        key_first, key_last = info[8 + 3 * back], info[8 + 3 * back + 1]
        return ((key_first <= a_last) & (key_last >= a_first)) | (
            (key_first <= b_last) & (key_last >= b_first)
        )

    def visit(chosen):
        keys, values = [], []
        for which in chosen:
            block = blocks[which]
            if len(block) == 2:
                packed = jnp.where(head == 0, block[0][...], block[1][...])
            else:
                packed = block[0][head]
            keys.append(packed[0:row_total])
            turned = [packed[at : at + HEAD] for at in range(row_total, 2 * row_total, HEAD)]
            values.append(jnp.concatenate([jnp.concatenate(turned, axis=1), ones], axis=0))
        keys, values = jnp.concatenate(keys, axis=0), jnp.concatenate(values, axis=1)
        chains = [slice(at, at + 256) for at in range(0, columns, 256)]
        scores = [matmul(keys, queries[:, cols]) for cols in chains]
        weights = []
        for score, cols in zip(scores, chains):
            masked = []
            for place, which in enumerate(chosen):
                part = score[place * row_total : (place + 1) * row_total]
                places = info[8 + 3 * backs[which] + 2] + lax.broadcasted_iota(jnp.int32, part.shape, 0)
                inside = (places >= span[0:1, cols]) & (places < span[1:2, cols])
                masked.append(jnp.where(inside, part, NEG))
            old = sums[0:1, cols]
            top = functools.reduce(
                jnp.maximum, [old] + [jnp.max(part, axis=0, keepdims=True) for part in masked]
            )
            sums[0:1, cols] = top
            parts = [jnp.exp2(part - top).astype(jnp.bfloat16) for part in masked]
            weights.append((jnp.concatenate(parts, axis=0), jnp.exp2(old - top)))
        for (weight, factor), cols in zip(weights, chains):
            summed = matmul(values, weight)
            sums[1:2, cols] = sums[1:2, cols] * factor + summed[HEAD : HEAD + 1]
            state[:, cols] = state[:, cols] * factor + summed[0:HEAD]

    needed = [meets(back) for back in backs]
    for count in range(1, len(backs) + 1):
        for chosen in itertools.combinations(range(len(backs)), count):
            only = functools.reduce(
                jnp.logical_and,
                [need if which in chosen else jnp.logical_not(need) for which, need in enumerate(needed)],
            )

            @pl.when(only)
            def _(chosen=chosen):
                visit(chosen)

    if last:
        mass = sums[1:2, :]
        some = mass > 0.0
        filled = jnp.where(some, mass, 1.0)
        result = (state[...] * (1.0 / filled)).astype(jnp.bfloat16)
        logs = jnp.where(some, sums[0:1, :] + jnp.log2(filled), START)
        high = logs.astype(jnp.bfloat16).astype(jnp.float32)
        index = lax.broadcasted_iota(jnp.int32, (TAIL, columns), 0)
        tail = jnp.where(index == 0, high, logs - high).astype(jnp.bfloat16)
        for group, out in enumerate(outs):
            cols = slice(group % 2 * row_total, group % 2 * row_total + row_total)

            @pl.when(pair == group // 2)
            def _(out=out, cols=cols):
                out[0:HEAD, :] = result[:, cols]
                out[HEAD : HEAD + TAIL, :] = tail[:, cols]


def attend(info, queries, spans, blocks, state, last=False):
    first = state is None
    pairs, heads, _, columns = queries.shape
    row_total = columns // 2
    per_query = lambda rows: pl.BlockSpec((None, None, rows, columns), lambda p, h, s: (p, h, 0, 0))
    in_specs = [per_query(HEAD), pl.BlockSpec((None, 8, columns), lambda p, h, s: (p, 0, 0))]
    operands = [queries, spans]
    for arrays in blocks.values():
        in_specs += [whole(array.shape) for array in arrays]
        operands += list(arrays)
    if not first:
        in_specs += [per_query(HEAD), per_query(8)]
        operands += list(state)
    scratch = []
    if last:
        def place(pair):
            def index(p, h, s):
                return (jnp.where(p == pair, h, jnp.where(p < pair, 0, heads - 1)), 0, 0)

            return index

        out_shape = [jax.ShapeDtypeStruct((heads, HEAD + TAIL, row_total), jnp.bfloat16)] * SEQ_Y
        out_specs = [
            pl.BlockSpec((None, HEAD + TAIL, row_total), place(group // 2)) for group in range(SEQ_Y)
        ]
        scratch = [pltpu.VMEM((HEAD, columns), jnp.float32), pltpu.VMEM((8, columns), jnp.float32)]
    else:
        out_shape = [
            jax.ShapeDtypeStruct((pairs, heads, HEAD, columns), jnp.float32),
            jax.ShapeDtypeStruct((pairs, heads, 8, columns), jnp.float32),
        ]
        out_specs = [per_query(HEAD), per_query(8)]
    flops = ATTEND_FLOPS * len(blocks)
    return pl.pallas_call(
        functools.partial(attend_kernel, first, last, tuple(blocks)),
        grid_spec=pltpu.PrefetchScalarGridSpec(
            num_scalar_prefetch=1,
            grid=(pairs, heads),
            in_specs=in_specs,
            out_specs=out_specs,
            scratch_shapes=scratch,
        ),
        out_shape=out_shape,
        compiler_params=pltpu.CompilerParams(vmem_limit_bytes=48 * 2**20),
        cost_estimate=pl.CostEstimate(flops=flops, bytes_accessed=2**20, transcendentals=0),
    )(info, *operands)


def merge_kernel(*refs):
    out, parts = refs[-1], refs[:-1]
    for head in range(parts[0].shape[0]):
        logs = []
        for part in parts:
            tail = part[head, HEAD : HEAD + TAIL, :].astype(jnp.float32)
            logs.append(tail[0:1] + tail[1:2])
        top = functools.reduce(jnp.maximum, logs)
        shares = [jnp.exp2(log - top) for log in logs]
        scale = 1.0 / functools.reduce(jnp.add, shares)
        total = functools.reduce(
            jnp.add,
            [part[head, 0:HEAD, :].astype(jnp.float32) * (share * scale) for part, share in zip(parts, shares)],
        )
        out[:, head * HEAD : (head + 1) * HEAD] = total.T.astype(jnp.bfloat16)


def merge(parts):
    heads, rows, row_total = parts[0].shape
    return pl.pallas_call(
        merge_kernel,
        grid=(1,),
        in_specs=[whole(parts[0].shape)] * len(parts),
        out_specs=whole((row_total, heads * HEAD)),
        out_shape=jax.ShapeDtypeStruct((row_total, heads * HEAD), jnp.bfloat16),
        compiler_params=pltpu.CompilerParams(vmem_limit_bytes=40 * 2**20),
        cost_estimate=pl.CostEstimate(flops=10**6, bytes_accessed=2**20, transcendentals=0),
    )(*parts)


def output_kernel(where, *refs):
    out = refs[-1]
    count = (len(refs) - 1) // 2
    total = matmul(refs[0][...], refs[count][...])
    for rows, weight in zip(refs[1:count], refs[count + 1 : -1]):
        total = total + matmul(rows[...], weight[...])
    out[...] = total.astype(out.dtype)


def output(where, rows, weights, other, dtype):
    row_total, deep = rows[0].shape
    columns = weights[0].shape[1] // 2

    def side(i, where):
        return (0, 1 - where[2] if other else where[2])

    return pl.pallas_call(
        output_kernel,
        grid_spec=pltpu.PrefetchScalarGridSpec(
            num_scalar_prefetch=1,
            grid=(1,),
            in_specs=[whole((row_total, deep))] * len(rows)
            + [pl.BlockSpec((deep, columns), side)] * len(weights),
            out_specs=whole((row_total, columns)),
        ),
        out_shape=jax.ShapeDtypeStruct((row_total, columns), dtype),
        compiler_params=pltpu.CompilerParams(vmem_limit_bytes=40 * 2**20),
        cost_estimate=pl.CostEstimate(flops=3 * 10**8, bytes_accessed=2 * 2**20, transcendentals=0),
    )(where, *rows, *weights)


def per_device(
    tokens,
    query_weight,
    key_weight,
    value_weight,
    output_weight,
    adapter_down_maps,
    adapter_up_maps,
    request_lengths,
    request_adapter,
    adapter_slot,
):
    row_count = tokens.shape[0]
    col_count = query_weight.shape[1]
    slots_here = adapter_down_maps.shape[0]
    cache = lax.axis_index("cache")
    places = jnp.stack([lax.axis_index("seq"), cache, lax.axis_index("mp")]).astype(jnp.int32)
    where = jnp.concatenate([places, request_lengths, request_adapter, adapter_slot])

    ups = adapter_up_maps.reshape(-1, adapter_up_maps.shape[3])
    messages = lower(where, tokens, adapter_down_maps, ups, col_count)
    tokens, *messages = lax.optimization_barrier((tokens, *messages))
    messages = [messages[0]] + [lax.ppermute(messages[s], "cache", around_x(s)) for s in (1, 2, 3)]
    key, value = project(tokens, key_weight, value_weight)
    tokens, key = lax.optimization_barrier((tokens, key))
    query, spans, info = project_query(where, tokens, query_weight)
    groups = [query] + [lax.ppermute(query, "seq", around_y(s)) for s in (1, 2, 3)]
    queries = jnp.stack([jnp.concatenate(groups[0:2], axis=2), jnp.concatenate(groups[2:4], axis=2)])
    packed = adapt(where, key, value, messages, slots_here)

    output_weight, _ = lax.optimization_barrier((output_weight, packed))
    chip_cols = output_weight.shape[1] // CACHE

    def columns(step):
        return lax.dynamic_slice_in_dim(output_weight, (cache + step) % CACHE * chip_cols, chip_cols, 1)

    weights = [columns(0)] + [lax.ppermute(columns(s), "cache", around_x(s)) for s in (1, 2, 3)]

    def ring(right, left):
        return lax.ppermute(right, "seq", around_z(1)), lax.ppermute(left, "seq", around_z(-1))

    half = SEQ_Z // 2
    right_1, left_1 = ring(packed, packed)
    state = attend(info, queries, spans, {0: (packed,)}, None)
    state, right_1, left_1 = lax.optimization_barrier((state, right_1, left_1))
    right_2, left_2 = ring(right_1, left_1)
    state = attend(info, queries, spans, {1: (right_1,), SEQ_Z - 1: (left_1,)}, state)
    state, right_2, left_2 = lax.optimization_barrier((state, right_2, left_2))
    right_3, left_3 = ring(right_2, left_2)
    state = attend(info, queries, spans, {2: (right_2,), SEQ_Z - 2: (left_2,)}, state)
    state, right_3, left_3 = lax.optimization_barrier((state, right_3, left_3))
    far = ring(right_3[0], left_3[1])
    state = attend(info, queries, spans, {3: (right_3,), SEQ_Z - 3: (left_3,)}, state)
    parts = attend(info, queries, spans, {half: far}, state, last=True)

    parts = [parts[0]] + [lax.ppermute(parts[g], "seq", around_y(-g)) for g in (2, 1, 3)]
    *parts, weights[1], weights[2], weights[3] = lax.optimization_barrier((*parts, *weights[1:]))
    attended = merge(parts)
    rows = [attended] + [lax.ppermute(attended, "cache", around_x(s)) for s in (1, 2, 3)]
    theirs = output(where, rows, weights, True, jnp.bfloat16)
    theirs = lax.ppermute(theirs, "mp", [(0, 1), (1, 0)])
    mine = output(where, rows, weights, False, jnp.float32)
    return (mine + theirs.astype(jnp.float32)).astype(jnp.bfloat16)


def solution(mesh):
    placed = (
        P("seq", None),
        P(None, ("cache", "mp")),
        P(None, ("cache", "mp")),
        P(None, ("cache", "mp")),
        P(("cache", "mp"), None),
        P("cache", None, None),
        P("cache", None, None, None),
        P(),
        P(),
        P(),
    )
    return jax.shard_map(
        per_device, mesh=mesh, in_specs=placed, out_specs=P("seq", ("cache", "mp")), check_vma=False
    )
```

profile of v0, /device:TPU:25, one launch (start us, length us, event | category | flops | bytes accessed | tf_op | source)
XLA Modules:
  0.0 98.2 jit_solution(4793741590958823176)
XLA Ops:
  1.3 4.9 %shard_map.100 = (bf16[896,128]{1,0:T(8,128)(2,1)}, bf16[896,128]{1,0:T(8,128)(2,1)}, bf16[896,128]{1,0:T(8,128)(2,1)}, bf16[896,128]{1,0:T(8,128)(2,1)}) custom-call(s32[43]{0:T(128)} %concatenate.9.where, bf16[384,3072]{1,0:T(8,128)(2,1)} %tokens.3, bf16[2,3072,128]{2,1,0:T(8,128)(2,1)} %down.1, bf16[256,2048]{1,0:T(8,128)(2,1)} %bitcast.12), custom_call_target="tpu_custom_call" | custom-call | flops 600000000 | bytes 6291456 | tf_op jit(solution)/shard_map/pallas_call | solution.py:123
  7.6 2.4 %collective-permute-start.4 = (bf16[896,128]{1,0:T(8,128)(2,1)}, bf16[896,128]{1,0:T(8,128)(2,1)S(1)}, u32[]{:S(2)}, u32[]{:S(2)}) collective-permute-start(bf16[896,128]{1,0:T(8,128)(2,1)} %get-tuple-element.67), channel_id=1, source_target_pairs={{0,4},{2,6},{4,0},{6,2},{1,5},{3,7},{5,1},{7,3},{8,12},{10,14},{12... | collective-permute-start | bytes 688136 | tf_op jit(solution)/shard_map/ppermute | solution.py:533
  11.2 1.7 %copy-done = bf16[384,3072]{1,0:T(8,128)(2,1)S(1)} copy-done((bf16[384,3072]{1,0:T(8,128)(2,1)S(1)}, bf16[384,3072]{1,0:T(8,128)(2,1)}, u32[]{:S(2)}) %copy-start) | copy-done | bytes 2359320
  14.2 2.1 %shard_map.101 = (f32[384,256]{1,0:T(8,128)S(1)}, f32[384,256]{1,0:T(8,128)S(1)}) custom-call(bf16[384,3072]{1,0:T(8,128)(2,1)S(1)} %copy-done, bf16[3072,256]{1,0:T(8,128)(2,1)S(1)} %copy-done.2, bf16[3072,256]{1,0:T(8,128)(2,1)S(1)} %copy-done.3), custom_call_target="tpu_custom_call" | custom-call | flops 1200000000 | bytes 6291456 | tf_op jit(solution)/shard_map/pallas_call | solution.py:247
  16.4 3.2 %shard_map.102 = (bf16[2,128,384]{2,1,0:T(8,128)(2,1)S(1)}, s32[2,8,768]{2,1,0:T(8,128)S(1)}, s32[32]{0:T(128)S(1)}) custom-call(s32[43]{0:T(128)S(1)} %copy-done.6, bf16[384,3072]{1,0:T(8,128)(2,1)S(1)} %copy-done.1, bf16[3072,256]{1,0:T(8,128)(2,1)S(1)} %copy-done.4), custom_call_target="tpu_custom_call" | custom-call | flops 600000000 | bytes 4194304 | tf_op jit(solution)/shard_map/pallas_call | solution.py:200
  19.7 2.2 %collective-permute-start.1 = (bf16[2,128,384]{2,1,0:T(8,128)(2,1)S(1)}, bf16[2,128,384]{2,1,0:T(8,128)(2,1)S(1)}, u32[]{:S(2)}, u32[]{:S(2)}) collective-permute-start(bf16[2,128,384]{2,1,0:T(8,128)(2,1)S(1)} %get-tuple-element.61), channel_id=1, source_target_pairs={{0,16},{8,24},{16,0},{24,8},{32,48},{40,56},{48,32},{56,40},{64,80... | collective-permute-start | bytes 589832 | tf_op jit(solution)/shard_map/ppermute | solution.py:537
  21.9 1.8 %shard_map.103.refs_0_ = bf16[2,768,128]{2,1,0:T(8,128)(2,1)S(1)} custom-call(s32[43]{0:T(128)S(1)} %copy-done.6, f32[384,256]{1,0:T(8,128)S(1)} %get-tuple-element.63.key, f32[384,256]{1,0:T(8,128)S(1)} %get-tuple-element.64.value, bf16[896,128]{1,0:T(8,128)(2,1)S(1)} %copy-done.5, bf16[896,128]{1,0:T(8,128)(2,1)S(1)} %collective-permute-done.3.refs_1_, ...), custom_call_target="tpu_custom_call" | custom-call | flops 400000000 | bytes 2097152 | tf_op jit(solution)/shard_map/pallas_call | solution.py:290
  23.8 1.7 %collective-permute-start.6 = (bf16[2,768,128]{2,1,0:T(8,128)(2,1)S(1)}, bf16[2,768,128]{2,1,0:T(8,128)(2,1)S(1)}, u32[]{:S(2)}, u32[]{:S(2)}) collective-permute-start(bf16[2,768,128]{2,1,0:T(8,128)(2,1)S(1)} %shard_map.103.refs_0_), channel_id=1, source_target_pairs={{0,32},{8,40},{16,48},{24,56},{32,64},{40,72},{48,80},{56,88},{64,... | collective-permute-start | bytes 1179656 | tf_op jit(solution)/shard_map/ppermute | solution.py:550
  25.5 4.0 %collective-permute-start.7 = (bf16[2,768,128]{2,1,0:T(8,128)(2,1)S(1)}, bf16[2,768,128]{2,1,0:T(8,128)(2,1)S(1)}, u32[]{:S(2)}, u32[]{:S(2)}) collective-permute-start(bf16[2,768,128]{2,1,0:T(8,128)(2,1)S(1)} %shard_map.103.refs_0_), channel_id=1, source_target_pairs={{0,224},{8,232},{16,240},{24,248},{32,0},{40,8},{48,16},{56,24},{6... | collective-permute-start | bytes 1179656 | tf_op jit(solution)/shard_map/ppermute | solution.py:550
  31.3 2.2 %shard_map.104 = (f32[2,2,128,768]{3,2,1,0:T(8,128)S(1)}, f32[2,2,8,768]{3,2,1,0:T(8,128)S(1)}) custom-call(s32[32]{0:T(128)S(1)} %get-tuple-element.60.info, bf16[2,2,128,768]{3,2,1,0:T(8,128)(2,1)S(1)} %pad_maximum_fusion.queries, s32[2,8,768]{2,1,0:T(8,128)S(1)} %get-tuple-element.62.span, bf16[2,768,128]{2,1,0:T(8,128)(2,1)S(1)} %shard_map.103.refs_0_), custom_call_target="tpu_custom_call" | custom-call | flops 1000000000 | bytes 1048576 | tf_op jit(solution)/shard_map/pallas_call | solution.py:435
  33.4 3.3 %collective-permute-done.6.refs_0_ = bf16[2,768,128]{2,1,0:T(8,128)(2,1)S(1)} collective-permute-done((bf16[2,768,128]{2,1,0:T(8,128)(2,1)S(1)}, bf16[2,768,128]{2,1,0:T(8,128)(2,1)S(1)}, u32[]{:S(2)}, u32[]{:S(2)}) %collective-permute-start.6) | collective-permute-done | bytes 393248 | tf_op jit(solution)/shard_map/ppermute | solution.py:550
  36.8 2.7 %collective-permute-start.9 = (bf16[2,768,128]{2,1,0:T(8,128)(2,1)S(1)}, bf16[2,768,128]{2,1,0:T(8,128)(2,1)S(1)}, u32[]{:S(2)}, u32[]{:S(2)}) collective-permute-start(bf16[2,768,128]{2,1,0:T(8,128)(2,1)S(1)} %collective-permute-done.7.refs_1_), channel_id=1, source_target_pairs={{0,224},{8,232},{16,240},{24,248},{32,0},{40,8},{48,16},{56,24},{6... | collective-permute-start | bytes 1179656 | tf_op jit(solution)/shard_map/ppermute | solution.py:550
  41.4 4.4 %collective-permute-done.8.refs_0_ = bf16[2,768,128]{2,1,0:T(8,128)(2,1)S(1)} collective-permute-done((bf16[2,768,128]{2,1,0:T(8,128)(2,1)S(1)}, bf16[2,768,128]{2,1,0:T(8,128)(2,1)S(1)}, u32[]{:S(2)}, u32[]{:S(2)}) %collective-permute-start.8) | collective-permute-done | bytes 393248 | tf_op jit(solution)/shard_map/ppermute | solution.py:550
  47.0 1.6 %collective-permute-start.11 = (bf16[2,768,128]{2,1,0:T(8,128)(2,1)S(1)}, bf16[2,768,128]{2,1,0:T(8,128)(2,1)S(1)}, u32[]{:S(2)}, u32[]{:S(2)}) collective-permute-start(bf16[2,768,128]{2,1,0:T(8,128)(2,1)S(1)} %collective-permute-done.9.refs_1_), channel_id=1, source_target_pairs={{0,224},{8,232},{16,240},{24,248},{32,0},{40,8},{48,16},{56,24},{6... | collective-permute-start | bytes 1179656 | tf_op jit(solution)/shard_map/ppermute | solution.py:550
  51.3 2.7 %collective-permute-done.10.refs_0_ = bf16[2,768,128]{2,1,0:T(8,128)(2,1)S(1)} collective-permute-done((bf16[2,768,128]{2,1,0:T(8,128)(2,1)S(1)}, bf16[2,768,128]{2,1,0:T(8,128)(2,1)S(1)}, u32[]{:S(2)}, u32[]{:S(2)}) %collective-permute-start.10) | collective-permute-done | bytes 393248 | tf_op jit(solution)/shard_map/ppermute | solution.py:550
  54.1 4.9 %collective-permute-start.12 = (bf16[768,128]{1,0:T(8,128)(2,1)S(1)}, bf16[768,128]{1,0:T(8,128)(2,1)S(1)}, u32[]{:S(2)}, u32[]{:S(2)}) collective-permute-start(bf16[768,128]{1,0:T(8,128)(2,1)S(1)} %slice_bitcast_fusion.1), channel_id=1, source_target_pairs={{0,32},{8,40},{16,48},{24,56},{32,64},{40,72},{48,80},{56,88},{64,... | collective-permute-start | bytes 589832 | tf_op jit(solution)/shard_map/ppermute | solution.py:550
  59.6 3.5 %collective-permute-start.19 = (bf16[256,768]{1,0:T(8,128)(2,1)S(1)}, bf16[256,768]{1,0:T(8,128)(2,1)S(1)}, u32[]{:S(2)}, u32[]{:S(2)}) collective-permute-start(bf16[256,768]{1,0:T(8,128)(2,1)S(1)} %get-tuple-element.102), channel_id=1, source_target_pairs={{0,6},{2,0},{4,2},{6,4},{1,7},{3,1},{5,3},{7,5},{8,14},{10,8},{12,... | collective-permute-start | bytes 1179656 | tf_op jit(solution)/shard_map/ppermute | solution.py:547
  65.3 2.7 %collective-permute-start.16 = (bf16[2,144,384]{2,1,0:T(8,128)(2,1)S(1)}, bf16[2,144,384]{2,1,0:T(8,128)(2,1)S(1)}, u32[]{:S(2)}, u32[]{:S(2)}) collective-permute-start(bf16[2,144,384]{2,1,0:T(8,128)(2,1)S(1)} %get-tuple-element.92), channel_id=1, source_target_pairs={{0,8},{8,16},{16,24},{24,0},{32,40},{40,48},{48,56},{56,32},{64,72... | collective-permute-start | bytes 663560 | tf_op jit(solution)/shard_map/ppermute | solution.py:566
  67.9 3.6 %collective-permute-done.18.refs_6_ = bf16[256,768]{1,0:T(8,128)(2,1)S(1)} collective-permute-done((bf16[256,768]{1,0:T(8,128)(2,1)S(1)}, bf16[256,768]{1,0:T(8,128)(2,1)S(1)}, u32[]{:S(2)}, u32[]{:S(2)}) %collective-permute-start.18) | collective-permute-done | bytes 393248 | tf_op jit(solution)/shard_map/ppermute | solution.py:547
  71.6 8.4 %collective-permute-done.19.refs_7_ = bf16[256,768]{1,0:T(8,128)(2,1)S(1)} collective-permute-done((bf16[256,768]{1,0:T(8,128)(2,1)S(1)}, bf16[256,768]{1,0:T(8,128)(2,1)S(1)}, u32[]{:S(2)}, u32[]{:S(2)}) %collective-permute-start.19) | collective-permute-done | bytes 393248 | tf_op jit(solution)/shard_map/ppermute | solution.py:547
  81.5 3.4 %collective-permute-start.21 = (bf16[384,256]{1,0:T(8,128)(2,1)S(1)}, bf16[384,256]{1,0:T(8,128)(2,1)S(1)}, u32[]{:S(2)}, u32[]{:S(2)}) collective-permute-start(bf16[384,256]{1,0:T(8,128)(2,1)S(1)} %shard_map.109.refs_0_), channel_id=1, source_target_pairs={{0,4},{2,6},{4,0},{6,2},{1,5},{3,7},{5,1},{7,3},{8,12},{10,14},{12... | collective-permute-start | bytes 589832 | tf_op jit(solution)/shard_map/ppermute | solution.py:569
  84.9 2.3 %collective-permute-done.20.refs_1_ = bf16[384,256]{1,0:T(8,128)(2,1)S(1)} collective-permute-done((bf16[384,256]{1,0:T(8,128)(2,1)S(1)}, bf16[384,256]{1,0:T(8,128)(2,1)S(1)}, u32[]{:S(2)}, u32[]{:S(2)}) %collective-permute-start.20) | collective-permute-done | bytes 196640 | tf_op jit(solution)/shard_map/ppermute | solution.py:569
  87.2 6.0 %collective-permute-done.21.refs_2_ = bf16[384,256]{1,0:T(8,128)(2,1)S(1)} collective-permute-done((bf16[384,256]{1,0:T(8,128)(2,1)S(1)}, bf16[384,256]{1,0:T(8,128)(2,1)S(1)}, u32[]{:S(2)}, u32[]{:S(2)}) %collective-permute-start.21) | collective-permute-done | bytes 196640 | tf_op jit(solution)/shard_map/ppermute | solution.py:569
  94.4 1.8 %collective-permute-start.23 = (bf16[384,384]{1,0:T(8,128)(2,1)S(1)}, bf16[384,384]{1,0:T(8,128)(2,1)S(1)}, u32[]{:S(2)}, u32[]{:S(2)}) collective-permute-start(bf16[384,384]{1,0:T(8,128)(2,1)S(1)} %shard_map.111), channel_id=1, source_target_pairs={{0,1},{1,0},{2,3},{3,2},{4,5},{5,4},{6,7},{7,6},{8,9},{9,8},{10,11... | collective-permute-start | bytes 884744 | tf_op jit(solution)/shard_map/ppermute | solution.py:571
  (62 shorter events, 20.3 us)
Async XLA Ops:
  6.3 15.6 %collective-permute-start.3 = (bf16[896,128]{1,0:T(8,128)(2,1)}, bf16[896,128]{1,0:T(8,128)(2,1)S(1)}, u32[]{:S(2)}, u32[]{:S(2)}) collective-permute-start(bf16[896,128]{1,0:T(8,128)(2,1)} %get-tuple-element.66), channel_id=1, source_target_pairs={{0,2},{2,4},{4,6},{6,0},{1,3},{3,5},{5,7},{7,1},{8,10},{10,12},{12... | collective-permute-start | bytes 688136 | tf_op jit(solution)/shard_map/ppermute | solution.py:533
  7.6 14.4 %collective-permute-start.4 = (bf16[896,128]{1,0:T(8,128)(2,1)}, bf16[896,128]{1,0:T(8,128)(2,1)S(1)}, u32[]{:S(2)}, u32[]{:S(2)}) collective-permute-start(bf16[896,128]{1,0:T(8,128)(2,1)} %get-tuple-element.67), channel_id=1, source_target_pairs={{0,4},{2,6},{4,0},{6,2},{1,5},{3,7},{5,1},{7,3},{8,12},{10,14},{12... | collective-permute-start | bytes 688136 | tf_op jit(solution)/shard_map/ppermute | solution.py:533
  10.0 11.9 %collective-permute-start.5 = (bf16[896,128]{1,0:T(8,128)(2,1)}, bf16[896,128]{1,0:T(8,128)(2,1)S(1)}, u32[]{:S(2)}, u32[]{:S(2)}) collective-permute-start(bf16[896,128]{1,0:T(8,128)(2,1)} %get-tuple-element.68), channel_id=1, source_target_pairs={{0,6},{2,0},{4,2},{6,4},{1,7},{3,1},{5,3},{7,5},{8,14},{10,8},{12,... | collective-permute-start | bytes 688136 | tf_op jit(solution)/shard_map/ppermute | solution.py:533
  19.6 9.9 %collective-permute-start = (bf16[2,128,384]{2,1,0:T(8,128)(2,1)S(1)}, bf16[2,128,384]{2,1,0:T(8,128)(2,1)S(1)}, u32[]{:S(2)}, u32[]{:S(2)}) collective-permute-start(bf16[2,128,384]{2,1,0:T(8,128)(2,1)S(1)} %get-tuple-element.61), channel_id=1, source_target_pairs={{0,8},{8,16},{16,24},{24,0},{32,40},{40,48},{48,56},{56,32},{64,72... | collective-permute-start | bytes 589832 | tf_op jit(solution)/shard_map/ppermute | solution.py:537
  19.7 9.9 %collective-permute-start.1 = (bf16[2,128,384]{2,1,0:T(8,128)(2,1)S(1)}, bf16[2,128,384]{2,1,0:T(8,128)(2,1)S(1)}, u32[]{:S(2)}, u32[]{:S(2)}) collective-permute-start(bf16[2,128,384]{2,1,0:T(8,128)(2,1)S(1)} %get-tuple-element.61), channel_id=1, source_target_pairs={{0,16},{8,24},{16,0},{24,8},{32,48},{40,56},{48,32},{56,40},{64,80... | collective-permute-start | bytes 589832 | tf_op jit(solution)/shard_map/ppermute | solution.py:537
  21.9 9.2 %collective-permute-start.2 = (bf16[2,128,384]{2,1,0:T(8,128)(2,1)S(1)}, bf16[2,128,384]{2,1,0:T(8,128)(2,1)S(1)}, u32[]{:S(2)}, u32[]{:S(2)}) collective-permute-start(bf16[2,128,384]{2,1,0:T(8,128)(2,1)S(1)} %get-tuple-element.61), channel_id=1, source_target_pairs={{0,24},{8,0},{16,8},{24,16},{32,56},{40,32},{48,40},{56,48},{64,88... | collective-permute-start | bytes 589832 | tf_op jit(solution)/shard_map/ppermute | solution.py:537
  23.8 13.0 %collective-permute-start.6 = (bf16[2,768,128]{2,1,0:T(8,128)(2,1)S(1)}, bf16[2,768,128]{2,1,0:T(8,128)(2,1)S(1)}, u32[]{:S(2)}, u32[]{:S(2)}) collective-permute-start(bf16[2,768,128]{2,1,0:T(8,128)(2,1)S(1)} %shard_map.103.refs_0_), channel_id=1, source_target_pairs={{0,32},{8,40},{16,48},{24,56},{32,64},{40,72},{48,80},{56,88},{64,... | collective-permute-start | bytes 1179656 | tf_op jit(solution)/shard_map/ppermute | solution.py:550
  25.5 11.3 %collective-permute-start.7 = (bf16[2,768,128]{2,1,0:T(8,128)(2,1)S(1)}, bf16[2,768,128]{2,1,0:T(8,128)(2,1)S(1)}, u32[]{:S(2)}, u32[]{:S(2)}) collective-permute-start(bf16[2,768,128]{2,1,0:T(8,128)(2,1)S(1)} %shard_map.103.refs_0_), channel_id=1, source_target_pairs={{0,224},{8,232},{16,240},{24,248},{32,0},{40,8},{48,16},{56,24},{6... | collective-permute-start | bytes 1179656 | tf_op jit(solution)/shard_map/ppermute | solution.py:550
  36.8 9.1 %collective-permute-start.8 = (bf16[2,768,128]{2,1,0:T(8,128)(2,1)S(1)}, bf16[2,768,128]{2,1,0:T(8,128)(2,1)S(1)}, u32[]{:S(2)}, u32[]{:S(2)}) collective-permute-start(bf16[2,768,128]{2,1,0:T(8,128)(2,1)S(1)} %collective-permute-done.6.refs_0_), channel_id=1, source_target_pairs={{0,32},{8,40},{16,48},{24,56},{32,64},{40,72},{48,80},{56,88},{64,... | collective-permute-start | bytes 1179656 | tf_op jit(solution)/shard_map/ppermute | solution.py:550
  36.8 9.1 %collective-permute-start.9 = (bf16[2,768,128]{2,1,0:T(8,128)(2,1)S(1)}, bf16[2,768,128]{2,1,0:T(8,128)(2,1)S(1)}, u32[]{:S(2)}, u32[]{:S(2)}) collective-permute-start(bf16[2,768,128]{2,1,0:T(8,128)(2,1)S(1)} %collective-permute-done.7.refs_1_), channel_id=1, source_target_pairs={{0,224},{8,232},{16,240},{24,248},{32,0},{40,8},{48,16},{56,24},{6... | collective-permute-start | bytes 1179656 | tf_op jit(solution)/shard_map/ppermute | solution.py:550
  45.9 8.2 %collective-permute-start.10 = (bf16[2,768,128]{2,1,0:T(8,128)(2,1)S(1)}, bf16[2,768,128]{2,1,0:T(8,128)(2,1)S(1)}, u32[]{:S(2)}, u32[]{:S(2)}) collective-permute-start(bf16[2,768,128]{2,1,0:T(8,128)(2,1)S(1)} %collective-permute-done.8.refs_0_), channel_id=1, source_target_pairs={{0,32},{8,40},{16,48},{24,56},{32,64},{40,72},{48,80},{56,88},{64,... | collective-permute-start | bytes 1179656 | tf_op jit(solution)/shard_map/ppermute | solution.py:550
  47.0 7.1 %collective-permute-start.11 = (bf16[2,768,128]{2,1,0:T(8,128)(2,1)S(1)}, bf16[2,768,128]{2,1,0:T(8,128)(2,1)S(1)}, u32[]{:S(2)}, u32[]{:S(2)}) collective-permute-start(bf16[2,768,128]{2,1,0:T(8,128)(2,1)S(1)} %collective-permute-done.9.refs_1_), channel_id=1, source_target_pairs={{0,224},{8,232},{16,240},{24,248},{32,0},{40,8},{48,16},{56,24},{6... | collective-permute-start | bytes 1179656 | tf_op jit(solution)/shard_map/ppermute | solution.py:550
  50.2 15.1 %collective-permute-start.17 = (bf16[256,768]{1,0:T(8,128)(2,1)S(1)}, bf16[256,768]{1,0:T(8,128)(2,1)S(1)}, u32[]{:S(2)}, u32[]{:S(2)}) collective-permute-start(bf16[256,768]{1,0:T(8,128)(2,1)S(1)} %get-tuple-element.104), channel_id=1, source_target_pairs={{0,2},{2,4},{4,6},{6,0},{1,3},{3,5},{5,7},{7,1},{8,10},{10,12},{12... | collective-permute-start | bytes 1179656 | tf_op jit(solution)/shard_map/ppermute | solution.py:547
  54.1 9.7 %collective-permute-start.12 = (bf16[768,128]{1,0:T(8,128)(2,1)S(1)}, bf16[768,128]{1,0:T(8,128)(2,1)S(1)}, u32[]{:S(2)}, u32[]{:S(2)}) collective-permute-start(bf16[768,128]{1,0:T(8,128)(2,1)S(1)} %slice_bitcast_fusion.1), channel_id=1, source_target_pairs={{0,32},{8,40},{16,48},{24,56},{32,64},{40,72},{48,80},{56,88},{64,... | collective-permute-start | bytes 589832 | tf_op jit(solution)/shard_map/ppermute | solution.py:550
  59.0 4.9 %collective-permute-start.13 = (bf16[768,128]{1,0:T(8,128)(2,1)S(1)}, bf16[768,128]{1,0:T(8,128)(2,1)S(1)}, u32[]{:S(2)}, u32[]{:S(2)}) collective-permute-start(bf16[768,128]{1,0:T(8,128)(2,1)S(1)} %slice_bitcast_fusion), channel_id=1, source_target_pairs={{0,224},{8,232},{16,240},{24,248},{32,0},{40,8},{48,16},{56,24},{6... | collective-permute-start | bytes 589832 | tf_op jit(solution)/shard_map/ppermute | solution.py:550
  59.1 12.5 %collective-permute-start.18 = (bf16[256,768]{1,0:T(8,128)(2,1)S(1)}, bf16[256,768]{1,0:T(8,128)(2,1)S(1)}, u32[]{:S(2)}, u32[]{:S(2)}) collective-permute-start(bf16[256,768]{1,0:T(8,128)(2,1)S(1)} %get-tuple-element.103), channel_id=1, source_target_pairs={{0,4},{2,6},{4,0},{6,2},{1,5},{3,7},{5,1},{7,3},{8,12},{10,14},{12... | collective-permute-start | bytes 1179656 | tf_op jit(solution)/shard_map/ppermute | solution.py:547
  59.6 20.4 %collective-permute-start.19 = (bf16[256,768]{1,0:T(8,128)(2,1)S(1)}, bf16[256,768]{1,0:T(8,128)(2,1)S(1)}, u32[]{:S(2)}, u32[]{:S(2)}) collective-permute-start(bf16[256,768]{1,0:T(8,128)(2,1)S(1)} %get-tuple-element.102), channel_id=1, source_target_pairs={{0,6},{2,0},{4,2},{6,4},{1,7},{3,1},{5,3},{7,5},{8,14},{10,8},{12,... | collective-permute-start | bytes 1179656 | tf_op jit(solution)/shard_map/ppermute | solution.py:547
  64.9 15.1 %collective-permute-start.14 = (bf16[2,144,384]{2,1,0:T(8,128)(2,1)S(1)}, bf16[2,144,384]{2,1,0:T(8,128)(2,1)S(1)}, u32[]{:S(2)}, u32[]{:S(2)}) collective-permute-start(bf16[2,144,384]{2,1,0:T(8,128)(2,1)S(1)} %get-tuple-element.90), channel_id=1, source_target_pairs={{0,16},{8,24},{16,0},{24,8},{32,48},{40,56},{48,32},{56,40},{64,80... | collective-permute-start | bytes 663560 | tf_op jit(solution)/shard_map/ppermute | solution.py:566
  65.3 14.7 %collective-permute-start.15 = (bf16[2,144,384]{2,1,0:T(8,128)(2,1)S(1)}, bf16[2,144,384]{2,1,0:T(8,128)(2,1)S(1)}, u32[]{:S(2)}, u32[]{:S(2)}) collective-permute-start(bf16[2,144,384]{2,1,0:T(8,128)(2,1)S(1)} %get-tuple-element.91), channel_id=1, source_target_pairs={{0,24},{8,0},{16,8},{24,16},{32,56},{40,32},{48,40},{56,48},{64,88... | collective-permute-start | bytes 663560 | tf_op jit(solution)/shard_map/ppermute | solution.py:566
  65.3 14.7 %collective-permute-start.16 = (bf16[2,144,384]{2,1,0:T(8,128)(2,1)S(1)}, bf16[2,144,384]{2,1,0:T(8,128)(2,1)S(1)}, u32[]{:S(2)}, u32[]{:S(2)}) collective-permute-start(bf16[2,144,384]{2,1,0:T(8,128)(2,1)S(1)} %get-tuple-element.92), channel_id=1, source_target_pairs={{0,8},{8,16},{16,24},{24,0},{32,40},{40,48},{48,56},{56,32},{64,72... | collective-permute-start | bytes 663560 | tf_op jit(solution)/shard_map/ppermute | solution.py:566
  80.2 7.0 %collective-permute-start.20 = (bf16[384,256]{1,0:T(8,128)(2,1)S(1)}, bf16[384,256]{1,0:T(8,128)(2,1)S(1)}, u32[]{:S(2)}, u32[]{:S(2)}) collective-permute-start(bf16[384,256]{1,0:T(8,128)(2,1)S(1)} %shard_map.109.refs_0_), channel_id=1, source_target_pairs={{0,2},{2,4},{4,6},{6,0},{1,3},{3,5},{5,7},{7,1},{8,10},{10,12},{12... | collective-permute-start | bytes 589832 | tf_op jit(solution)/shard_map/ppermute | solution.py:569
  81.5 11.7 %collective-permute-start.21 = (bf16[384,256]{1,0:T(8,128)(2,1)S(1)}, bf16[384,256]{1,0:T(8,128)(2,1)S(1)}, u32[]{:S(2)}, u32[]{:S(2)}) collective-permute-start(bf16[384,256]{1,0:T(8,128)(2,1)S(1)} %shard_map.109.refs_0_), channel_id=1, source_target_pairs={{0,4},{2,6},{4,0},{6,2},{1,5},{3,7},{5,1},{7,3},{8,12},{10,14},{12... | collective-permute-start | bytes 589832 | tf_op jit(solution)/shard_map/ppermute | solution.py:569
  84.9 8.3 %collective-permute-start.22 = (bf16[384,256]{1,0:T(8,128)(2,1)S(1)}, bf16[384,256]{1,0:T(8,128)(2,1)S(1)}, u32[]{:S(2)}, u32[]{:S(2)}) collective-permute-start(bf16[384,256]{1,0:T(8,128)(2,1)S(1)} %shard_map.109.refs_0_), channel_id=1, source_target_pairs={{0,6},{2,0},{4,2},{6,4},{1,7},{3,1},{5,3},{7,5},{8,14},{10,8},{12,... | collective-permute-start | bytes 589832 | tf_op jit(solution)/shard_map/ppermute | solution.py:569
  94.4 3.0 %collective-permute-start.23 = (bf16[384,384]{1,0:T(8,128)(2,1)S(1)}, bf16[384,384]{1,0:T(8,128)(2,1)S(1)}, u32[]{:S(2)}, u32[]{:S(2)}) collective-permute-start(bf16[384,384]{1,0:T(8,128)(2,1)S(1)} %shard_map.111), channel_id=1, source_target_pairs={{0,1},{1,0},{2,3},{3,2},{4,5},{5,4},{6,7},{7,6},{8,9},{9,8},{10,11... | collective-permute-start | bytes 884744 | tf_op jit(solution)/shard_map/ppermute | solution.py:571
  (9 other events, 35.9 us)
where the time goes:
time: 98.8 us; the launch traced here: 98.2 us
  starting transfers between devices  37.2 us (38%)
  waiting for transfers between devices  32.6 us (33%)
  Pallas kernels  20.1 us (20%)
  local copies, waits for them, and re-layouts  7.2 us (7%)
    ppermute x3, waiting for transfers between devices, per_device(): lax.ppermute(columns(s), 'cache', around_x(s))  12 us
    ppermute x4, waiting for transfers between devices, ring(): lax.ppermute(right, 'seq', around_z(1))  10.5 us
    ppermute x4, starting transfers between devices, ring(): lax.ppermute(left, 'seq', around_z(-1))  8.4 us
    ppermute x3, waiting for transfers between devices, per_device(): lax.ppermute(attended, 'cache', around_x(s))  8.32 us
    ppermute x4, starting transfers between devices, ring(): lax.ppermute(right, 'seq', around_z(1))  7.65 us
    pallas_call x5, Pallas kernels, attend(): pl.pallas_call(functools.partial(attend_kernel, first, last, tuple(blocks...  5.48 us
    pallas_call x1, Pallas kernels, lower(): pl.pallas_call(lower_kernel, grid_spec=pltpu.PrefetchScalarGridSpec(num_s...  4.94 us
    ppermute x3, starting transfers between devices, per_device(): lax.ppermute(messages[s], 'cache', around_x(s))  4.89 us
  transfers between devices with their start and end apart: 24, of which 9 were waited for; matrix products, arithmetic and copies ran while one was open for 2% of the time, Pallas kernels for 14%

commit v1 on v0

--- a/solution.py
+++ b/solution.py
@@ -22,7 +22,7 @@
 
 
 CHUNKS = 6
-ATTEND_FLOPS = 10**9
+ATTEND_FLOPS = 10**6
 
 
 def around_z(step):
@@ -64,8 +64,42 @@
     return found
 
 
+def requests_met(where, row_total, spans, info):
+    bounds = request_ends(where)
+    seq = where[0]
+    seq_z, seq_y = lax.div(seq, SEQ_Y), lax.rem(seq, SEQ_Y)
+
+    def request_at(row):
+        found = jnp.int32(0)
+        for _, end in bounds:
+            found = found + (row >= end).astype(jnp.int32)
+        return found
+
+    def groups_row(group):
+        return (seq_z * SEQ_Y + lax.rem(seq_y + SEQ_Y - group, SEQ_Y)) * row_total
+
+    for group in range(SEQ_Y):
+        row = groups_row(group)
+        info[2 * group] = request_at(row)
+        info[2 * group + 1] = request_at(row + row_total - 1)
+        places = row + lax.broadcasted_iota(jnp.int32, (8, row_total), 1)
+        starts = jnp.zeros(places.shape, jnp.int32)
+        ends = jnp.zeros(places.shape, jnp.int32)
+        for start, end in bounds:
+            starts = jnp.where(places >= start, start, starts)
+            ends = jnp.where(places >= start, end, ends)
+        index = lax.broadcasted_iota(jnp.int32, (8, row_total), 0)
+        cols = slice(group % 2 * row_total, group % 2 * row_total + row_total)
+        spans[group // 2, :, cols] = jnp.where(index == 0, starts, ends)
+    for back in range(SEQ_Z):
+        row = (lax.rem(seq_z + SEQ_Z - back, SEQ_Z) * SEQ_Y + seq_y) * row_total
+        info[8 + 3 * back] = request_at(row)
+        info[8 + 3 * back + 1] = request_at(row + row_total - 1)
+        info[8 + 3 * back + 2] = row
+
+
 def lower_kernel(where, tokens, down, ups, *refs):
-    outs, (held, maps, columns, arrived) = refs[:CACHE], refs[CACHE:]
+    outs, (spans, info, held, maps, columns, arrived) = refs[:CACHE], refs[CACHE:]
     row_total, width = tokens.shape
     slot_total, _, low = down.shape
     up_rows = ups.shape[0]
@@ -91,6 +125,7 @@
             pltpu.make_async_copy(ups.at[:, pl.ds(first, col_count)], columns.at[step], arrived.at[CHUNKS * 4 + step])
         )
         up_copies[-1].start()
+    requests_met(where, row_total, spans, info)
     places = where[0] * row_total + lax.broadcasted_iota(jnp.int32, (row_total, low), 0)
     mine = slots_of_rows(places, where)
     total = None
@@ -126,7 +161,8 @@
             num_scalar_prefetch=1,
             grid=(1,),
             in_specs=[pl.BlockSpec(memory_space=pltpu.HBM)] * 3,
-            out_specs=[whole((out_rows, HEAD))] * CACHE,
+            out_specs=[whole((out_rows, HEAD))] * CACHE
+            + [whole((SEQ_Y // 2, 8, 2 * row_total)), pl.BlockSpec(memory_space=pltpu.SMEM)],
             scratch_shapes=[
                 pltpu.VMEM((CHUNKS, row_total, deep), jnp.bfloat16),
                 pltpu.VMEM((CHUNKS, slot_total, deep, low), jnp.bfloat16),
@@ -134,13 +170,17 @@
                 pltpu.SemaphoreType.DMA((CHUNKS * 4 + CACHE,)),
             ],
         ),
-        out_shape=[jax.ShapeDtypeStruct((out_rows, HEAD), jnp.bfloat16)] * CACHE,
+        out_shape=[jax.ShapeDtypeStruct((out_rows, HEAD), jnp.bfloat16)] * CACHE
+        + [
+            jax.ShapeDtypeStruct((SEQ_Y // 2, 8, 2 * row_total), jnp.int32),
+            jax.ShapeDtypeStruct((8 + 3 * SEQ_Z,), jnp.int32),
+        ],
         compiler_params=pltpu.CompilerParams(vmem_limit_bytes=62 * 2**20),
         cost_estimate=pl.CostEstimate(flops=6 * 10**8, bytes_accessed=6 * 2**20, transcendentals=0),
     )(where, tokens, down, ups)
 
 
-def query_kernel(steps, where, tokens, wq, query, spans, info, total):
+def query_kernel(steps, tokens, wq, query, total):
     step = pl.program_id(0)
     row_total = tokens.shape[0]
     held = tokens[...]
@@ -148,37 +188,6 @@
     @pl.when(step == 0)
     def _():
         total[...] = matmul(held, wq[...])
-        bounds = request_ends(where)
-        seq = where[0]
-        seq_z, seq_y = lax.div(seq, SEQ_Y), lax.rem(seq, SEQ_Y)
-
-        def request_at(row):
-            found = jnp.int32(0)
-            for _, end in bounds:
-                found = found + (row >= end).astype(jnp.int32)
-            return found
-
-        def groups_row(group):
-            return (seq_z * SEQ_Y + lax.rem(seq_y + SEQ_Y - group, SEQ_Y)) * row_total
-
-        for group in range(SEQ_Y):
-            row = groups_row(group)
-            info[2 * group] = request_at(row)
-            info[2 * group + 1] = request_at(row + row_total - 1)
-            places = row + lax.broadcasted_iota(jnp.int32, (8, row_total), 1)
-            starts = jnp.zeros(places.shape, jnp.int32)
-            ends = jnp.zeros(places.shape, jnp.int32)
-            for start, end in bounds:
-                starts = jnp.where(places >= start, start, starts)
-                ends = jnp.where(places >= start, end, ends)
-            index = lax.broadcasted_iota(jnp.int32, (8, row_total), 0)
-            cols = slice(group % 2 * row_total, group % 2 * row_total + row_total)
-            spans[group // 2, :, cols] = jnp.where(index == 0, starts, ends)
-        for back in range(SEQ_Z):
-            row = (lax.rem(seq_z + SEQ_Z - back, SEQ_Z) * SEQ_Y + seq_y) * row_total
-            info[8 + 3 * back] = request_at(row)
-            info[8 + 3 * back + 1] = request_at(row + row_total - 1)
-            info[8 + 3 * back + 2] = row
 
     @pl.when(step > 0)
     def _():
@@ -191,7 +200,7 @@
             query[head] = scaled[:, head * HEAD : (head + 1) * HEAD].T.astype(jnp.bfloat16)
 
 
-def project_query(where, tokens, wq):
+def project_query(tokens, wq):
     steps = 3
     row_total, width = tokens.shape
     col_count = wq.shape[1]
@@ -199,28 +208,17 @@
     deep = width // steps
     return pl.pallas_call(
         functools.partial(query_kernel, steps),
-        grid_spec=pltpu.PrefetchScalarGridSpec(
-            num_scalar_prefetch=1,
-            grid=(steps,),
-            in_specs=[
-                pl.BlockSpec((row_total, deep), lambda i, *rest: (0, i)),
-                pl.BlockSpec((deep, col_count), lambda i, *rest: (i, 0)),
-            ],
-            out_specs=[
-                whole((heads, HEAD, row_total)),
-                whole((SEQ_Y // 2, 8, 2 * row_total)),
-                pl.BlockSpec(memory_space=pltpu.SMEM),
-            ],
-            scratch_shapes=[pltpu.VMEM((row_total, col_count), jnp.float32)],
-        ),
-        out_shape=[
-            jax.ShapeDtypeStruct((heads, HEAD, row_total), jnp.bfloat16),
-            jax.ShapeDtypeStruct((SEQ_Y // 2, 8, 2 * row_total), jnp.int32),
-            jax.ShapeDtypeStruct((8 + 3 * SEQ_Z,), jnp.int32),
+        grid=(steps,),
+        in_specs=[
+            pl.BlockSpec((row_total, deep), lambda i: (0, i)),
+            pl.BlockSpec((deep, col_count), lambda i: (i, 0)),
         ],
+        out_specs=whole((heads, HEAD, row_total)),
+        scratch_shapes=[pltpu.VMEM((row_total, col_count), jnp.float32)],
+        out_shape=jax.ShapeDtypeStruct((heads, HEAD, row_total), jnp.bfloat16),
         compiler_params=pltpu.CompilerParams(vmem_limit_bytes=24 * 2**20),
         cost_estimate=pl.CostEstimate(flops=6 * 10**8, bytes_accessed=4 * 2**20, transcendentals=0),
-    )(where, tokens, wq)
+    )(tokens, wq)
 
 
 def project_kernel(tokens, wk, wv, key, value):
@@ -442,7 +440,7 @@
             scratch_shapes=scratch,
         ),
         out_shape=out_shape,
-        compiler_params=pltpu.CompilerParams(vmem_limit_bytes=48 * 2**20),
+        compiler_params=pltpu.CompilerParams(vmem_limit_bytes=24 * 2**20),
         cost_estimate=pl.CostEstimate(flops=flops, bytes_accessed=2**20, transcendentals=0),
     )(info, *operands)
 
@@ -524,16 +522,21 @@
     col_count = query_weight.shape[1]
     slots_here = adapter_down_maps.shape[0]
     cache = lax.axis_index("cache")
-    places = jnp.stack([lax.axis_index("seq"), cache, lax.axis_index("mp")]).astype(jnp.int32)
-    where = jnp.concatenate([places, request_lengths, request_adapter, adapter_slot])
+    known = [jnp.stack([lax.axis_index("seq"), cache, lax.axis_index("mp")]).astype(jnp.int32)]
+    known += [request_lengths, request_adapter, adapter_slot]
+    known_total = sum(array.shape[0] for array in known)
+    where, at = jnp.zeros((known_total,), jnp.int32), 0
+    for array in known:
+        where = where + jnp.pad(array, (at, known_total - at - array.shape[0]))
+        at = at + array.shape[0]
 
     ups = adapter_up_maps.reshape(-1, adapter_up_maps.shape[3])
-    messages = lower(where, tokens, adapter_down_maps, ups, col_count)
+    *messages, spans, info = lower(where, tokens, adapter_down_maps, ups, col_count)
     tokens, *messages = lax.optimization_barrier((tokens, *messages))
     messages = [messages[0]] + [lax.ppermute(messages[s], "cache", around_x(s)) for s in (1, 2, 3)]
     key, value = project(tokens, key_weight, value_weight)
     tokens, key = lax.optimization_barrier((tokens, key))
-    query, spans, info = project_query(where, tokens, query_weight)
+    query = project_query(tokens, query_weight)
     groups = [query] + [lax.ppermute(query, "seq", around_y(s)) for s in (1, 2, 3)]
     queries = jnp.stack([jnp.concatenate(groups[0:2], axis=2), jnp.concatenate(groups[2:4], axis=2)])
     packed = adapt(where, key, value, messages, slots_here)
@@ -552,19 +555,24 @@
     half = SEQ_Z // 2
     right_1, left_1 = ring(packed, packed)
     state = attend(info, queries, spans, {0: (packed,)}, None)
-    state, right_1, left_1 = lax.optimization_barrier((state, right_1, left_1))
+    right_1 = lax.optimization_barrier((state[0], right_1))[1]
+    left_1 = lax.optimization_barrier((state[0], left_1))[1]
     right_2, left_2 = ring(right_1, left_1)
     state = attend(info, queries, spans, {1: (right_1,), SEQ_Z - 1: (left_1,)}, state)
-    state, right_2, left_2 = lax.optimization_barrier((state, right_2, left_2))
+    right_2 = lax.optimization_barrier((state[0], right_2))[1]
+    left_2 = lax.optimization_barrier((state[0], left_2))[1]
     right_3, left_3 = ring(right_2, left_2)
+    state, weights[1] = lax.optimization_barrier((state, weights[1]))
     state = attend(info, queries, spans, {2: (right_2,), SEQ_Z - 2: (left_2,)}, state)
-    state, right_3, left_3 = lax.optimization_barrier((state, right_3, left_3))
+    right_3 = lax.optimization_barrier((state[0], right_3))[1]
+    left_3 = lax.optimization_barrier((state[0], left_3))[1]
     far = ring(right_3[0], left_3[1])
+    state, weights[3] = lax.optimization_barrier((state, weights[3]))
     state = attend(info, queries, spans, {3: (right_3,), SEQ_Z - 3: (left_3,)}, state)
     parts = attend(info, queries, spans, {half: far}, state, last=True)
 
     parts = [parts[0]] + [lax.ppermute(parts[g], "seq", around_y(-g)) for g in (2, 1, 3)]
-    *parts, weights[1], weights[2], weights[3] = lax.optimization_barrier((*parts, *weights[1:]))
+    *parts, weights[2] = lax.optimization_barrier((*parts, weights[2]))
     attended = merge(parts)
     rows = [attended] + [lax.ppermute(attended, "cache", around_x(s)) for s in (1, 2, 3)]
     theirs = output(where, rows, weights, True, jnp.bfloat16)

time: 98.8 us -> 98.6 us (level)
  the two profiles are of different devices: /device:TPU:25 before, /device:TPU:1 now
where the time goes in v1:
time: 98.6 us; the launch traced here: 98.7 us
  starting transfers between devices  41.5 us (42%)
  Pallas kernels  32.3 us (33%)
  waiting for transfers between devices  17.7 us (18%)
  local copies, waits for them, and re-layouts  4.59 us (5%)
  other arithmetic  2.34 us (2%)
    pallas_call x5, Pallas kernels, attend(): pl.pallas_call(functools.partial(attend_kernel, first, last, tuple(blocks...  19.2 us
    ppermute x4, starting transfers between devices, ring(): lax.ppermute(left, 'seq', around_z(-1))  12.4 us
    ppermute x1, starting transfers between devices, per_device(): theirs = lax.ppermute(theirs, 'mp', [(0, 1), (1, 0)])  9.35 us
    ppermute x3, waiting for transfers between devices, per_device(): lax.ppermute(parts[g], 'seq', around_y(-g))  7.1 us
    ppermute x3, starting transfers between devices, per_device(): lax.ppermute(messages[s], 'cache', around_x(s))  5.72 us
    ppermute x3, starting transfers between devices, per_device(): lax.ppermute(query, 'seq', around_y(s))  5.06 us
    pallas_call x1, Pallas kernels, lower(): pl.pallas_call(lower_kernel, grid_spec=pltpu.PrefetchScalarGridSpec(num_s...  4.98 us
    ppermute x3, starting transfers between devices, per_device(): lax.ppermute(attended, 'cache', around_x(s))  4.28 us
  transfers between devices with their start and end apart: 24, of which 10 were waited for; matrix products, arithmetic and copies ran while one was open for 2% of the time, Pallas kernels for 26%

profile of v1, /device:TPU:1, one launch (start us, length us, event | category | flops | bytes accessed | tf_op | source)
XLA Modules:
  0.0 98.7 jit_solution(13479332161719524330)
XLA Ops:
  1.4 5.0 %shard_map.100 = (bf16[896,128]{1,0:T(8,128)(2,1)}, bf16[896,128]{1,0:T(8,128)(2,1)}, bf16[896,128]{1,0:T(8,128)(2,1)}, bf16[896,128]{1,0:T(8,128)(2,1)}, s32[2,8,768]{2,1,0:T(8,128)}, /*index=5*/s32[32]{0:T(128)}) custom-call(s32[43]{0:T(128)} %pad_add_fusion.1.where, bf16[384,3072]{1,0:T(8,128)(2,1)} %tokens.3, bf16[2,3072,128]{2,1,0:T(8,128)(2,1)} %down.1, ...), custom_call_target="tpu_custom_call" | custom-call | flops 600000000 | bytes 6291456 | tf_op jit(solution)/shard_map/pallas_call | solution.py:158
  6.4 2.1 %collective-permute-start.3 = (bf16[896,128]{1,0:T(8,128)(2,1)}, bf16[896,128]{1,0:T(8,128)(2,1)S(1)}, u32[]{:S(2)}, u32[]{:S(2)}) collective-permute-start(bf16[896,128]{1,0:T(8,128)(2,1)} %get-tuple-element.62), channel_id=1, source_target_pairs={{0,2},{2,4},{4,6},{6,0},{1,3},{3,5},{5,7},{7,1},{8,10},{10,12},{12... | collective-permute-start | bytes 688136 | tf_op jit(solution)/shard_map/ppermute | solution.py:536
  8.5 2.5 %collective-permute-start.4 = (bf16[896,128]{1,0:T(8,128)(2,1)}, bf16[896,128]{1,0:T(8,128)(2,1)S(1)}, u32[]{:S(2)}, u32[]{:S(2)}) collective-permute-start(bf16[896,128]{1,0:T(8,128)(2,1)} %get-tuple-element.63), channel_id=1, source_target_pairs={{0,4},{2,6},{4,0},{6,2},{1,5},{3,7},{5,1},{7,3},{8,12},{10,14},{12... | collective-permute-start | bytes 688136 | tf_op jit(solution)/shard_map/ppermute | solution.py:536
  12.1 1.7 %copy-done = bf16[384,3072]{1,0:T(8,128)(2,1)S(1)} copy-done((bf16[384,3072]{1,0:T(8,128)(2,1)S(1)}, bf16[384,3072]{1,0:T(8,128)(2,1)}, u32[]{:S(2)}) %copy-start) | copy-done | bytes 2359320
  15.2 2.1 %shard_map.101 = (f32[384,256]{1,0:T(8,128)S(1)}, f32[384,256]{1,0:T(8,128)S(1)}) custom-call(bf16[384,3072]{1,0:T(8,128)(2,1)S(1)} %copy-done, bf16[3072,256]{1,0:T(8,128)(2,1)S(1)} %copy-done.1, bf16[3072,256]{1,0:T(8,128)(2,1)S(1)} %copy-done.2), custom_call_target="tpu_custom_call" | custom-call | flops 1200000000 | bytes 6291456 | tf_op jit(solution)/shard_map/pallas_call | solution.py:245
  17.3 1.6 %shard_map.102 = bf16[2,128,384]{2,1,0:T(8,128)(2,1)S(1)} custom-call(bf16[384,3072]{1,0:T(8,128)(2,1)S(1)} %copy-done, bf16[3072,256]{1,0:T(8,128)(2,1)S(1)} %copy-done.3), custom_call_target="tpu_custom_call" | custom-call | flops 600000000 | bytes 4194304 | tf_op jit(solution)/shard_map/pallas_call | solution.py:209
  20.3 2.6 %collective-permute-start.1 = (bf16[2,128,384]{2,1,0:T(8,128)(2,1)S(1)}, bf16[2,128,384]{2,1,0:T(8,128)(2,1)S(1)}, u32[]{:S(2)}, u32[]{:S(2)}) collective-permute-start(bf16[2,128,384]{2,1,0:T(8,128)(2,1)S(1)} %shard_map.102), channel_id=1, source_target_pairs={{0,16},{8,24},{16,0},{24,8},{32,48},{40,56},{48,32},{56,40},{64,80... | collective-permute-start | bytes 589832 | tf_op jit(solution)/shard_map/ppermute | solution.py:540
  24.0 1.8 %shard_map.103.refs_0_ = bf16[2,768,128]{2,1,0:T(8,128)(2,1)S(1)} custom-call(s32[43]{0:T(128)S(1)} %copy-done.6, f32[384,256]{1,0:T(8,128)S(1)} %get-tuple-element.59.key, f32[384,256]{1,0:T(8,128)S(1)} %get-tuple-element.60.value, bf16[896,128]{1,0:T(8,128)(2,1)S(1)} %copy-done.5, bf16[896,128]{1,0:T(8,128)(2,1)S(1)} %collective-permute-done.3.refs_1_, ...), custom_call_target="tpu_custom_call" | custom-call | flops 400000000 | bytes 2097152 | tf_op jit(solution)/shard_map/pallas_call | solution.py:288
  25.9 5.7 %collective-permute-start.7 = (bf16[2,768,128]{2,1,0:T(8,128)(2,1)S(1)}, bf16[2,768,128]{2,1,0:T(8,128)(2,1)S(1)}, u32[]{:S(2)}, u32[]{:S(2)}) collective-permute-start(bf16[2,768,128]{2,1,0:T(8,128)(2,1)S(1)} %shard_map.103.refs_0_), channel_id=1, source_target_pairs={{0,224},{8,232},{16,240},{24,248},{32,0},{40,8},{48,16},{56,24},{6... | collective-permute-start | bytes 1179656 | tf_op jit(solution)/shard_map/ppermute | solution.py:553
  31.8 3.6 %shard_map.104 = (f32[2,2,128,768]{3,2,1,0:T(8,128)S(1)}, f32[2,2,8,768]{3,2,1,0:T(8,128)S(1)}) custom-call(s32[32]{0:T(128)S(1)} %copy-done.7, bf16[2,2,128,768]{3,2,1,0:T(8,128)(2,1)S(1)} %pad_maximum_fusion.queries, s32[2,8,768]{2,1,0:T(8,128)S(1)} %copy-done.4, bf16[2,768,128]{2,1,0:T(8,128)(2,1)S(1)} %shard_map.103.refs_0_), custom_call_target="tpu_custom_call" | custom-call | flops 1000000 | bytes 1048576 | tf_op jit(solution)/shard_map/pallas_call | solution.py:433
  35.3 2.3 %collective-permute-done.7.refs_1_ = bf16[2,768,128]{2,1,0:T(8,128)(2,1)S(1)} collective-permute-done((bf16[2,768,128]{2,1,0:T(8,128)(2,1)S(1)}, bf16[2,768,128]{2,1,0:T(8,128)(2,1)S(1)}, u32[]{:S(2)}, u32[]{:S(2)}) %collective-permute-start.7) | collective-permute-done | bytes 393248 | tf_op jit(solution)/shard_map/ppermute | solution.py:553
  37.6 3.4 %collective-permute-start.9 = (bf16[2,768,128]{2,1,0:T(8,128)(2,1)S(1)}, bf16[2,768,128]{2,1,0:T(8,128)(2,1)}, u32[]{:S(2)}, u32[]{:S(2)}) collective-permute-start(bf16[2,768,128]{2,1,0:T(8,128)(2,1)S(1)} %collective-permute-done.7.refs_1_), channel_id=1, source_target_pairs={{0,224},{8,232},{16,240},{24,248},{32,0},{40,8},{48,16},{56,24},{6... | collective-permute-start | bytes 1179656 | tf_op jit(solution)/shard_map/ppermute | solution.py:553
  42.9 3.5 %shard_map.105 = (f32[2,2,128,768]{3,2,1,0:T(8,128)S(1)}, f32[2,2,8,768]{3,2,1,0:T(8,128)S(1)}) custom-call(s32[32]{0:T(128)S(1)} %copy-done.7, bf16[2,2,128,768]{3,2,1,0:T(8,128)(2,1)S(1)} %pad_maximum_fusion.queries, s32[2,8,768]{2,1,0:T(8,128)S(1)} %copy-done.4, bf16[2,768,128]{2,1,0:T(8,128)(2,1)S(1)} %collective-permute-done.6.refs_0_, ...), custom_call_target="tpu_custom_call" | custom-call | flops 2000000 | bytes 1048576 | tf_op jit(solution)/shard_map/pallas_call | solution.py:433
  46.4 3.2 %collective-permute-start.13 = (bf16[2,768,128]{2,1,0:T(8,128)(2,1)}, bf16[2,768,128]{2,1,0:T(8,128)(2,1)S(1)}, u32[]{:S(2)}, u32[]{:S(2)}) collective-permute-start(bf16[2,768,128]{2,1,0:T(8,128)(2,1)} %collective-permute-done.9.refs_1_), channel_id=1, source_target_pairs={{0,224},{8,232},{16,240},{24,248},{32,0},{40,8},{48,16},{56,24},{6... | collective-permute-start | bytes 1179656 | tf_op jit(solution)/shard_map/ppermute | solution.py:553
  50.9 4.7 %shard_map.106 = (f32[2,2,128,768]{3,2,1,0:T(8,128)S(1)}, f32[2,2,8,768]{3,2,1,0:T(8,128)S(1)}) custom-call(s32[32]{0:T(128)S(1)} %copy-done.7, bf16[2,2,128,768]{3,2,1,0:T(8,128)(2,1)S(1)} %pad_maximum_fusion.queries, s32[2,8,768]{2,1,0:T(8,128)S(1)} %copy-done.4, bf16[2,768,128]{2,1,0:T(8,128)(2,1)} %collective-permute-done.8.refs_0_, ...), custom_call_target="tpu_custom_call" | custom-call | flops 2000000 | bytes 1048576 | tf_op jit(solution)/shard_map/pallas_call | solution.py:433
  55.6 2.1 %collective-permute-done.11.refs_0_ = bf16[2,768,128]{2,1,0:T(8,128)(2,1)S(1)} collective-permute-done((bf16[2,768,128]{2,1,0:T(8,128)(2,1)}, bf16[2,768,128]{2,1,0:T(8,128)(2,1)S(1)}, u32[]{:S(2)}, u32[]{:S(2)}) %collective-permute-start.11) | collective-permute-done | bytes 393248 | tf_op jit(solution)/shard_map/ppermute | solution.py:553
  59.6 3.5 %shard_map.107 = (f32[2,2,128,768]{3,2,1,0:T(8,128)S(1)}, f32[2,2,8,768]{3,2,1,0:T(8,128)S(1)}) custom-call(s32[32]{0:T(128)S(1)} %copy-done.7, bf16[2,2,128,768]{3,2,1,0:T(8,128)(2,1)S(1)} %pad_maximum_fusion.queries, s32[2,8,768]{2,1,0:T(8,128)S(1)} %copy-done.4, bf16[2,768,128]{2,1,0:T(8,128)(2,1)S(1)} %collective-permute-done.11.refs_0_, ...), custom_call_target="tpu_custom_call" | custom-call | flops 2000000 | bytes 1048576 | tf_op jit(solution)/shard_map/pallas_call | solution.py:433
  64.8 3.9 %shard_map.108 = (bf16[2,144,384]{2,1,0:T(8,128)(2,1)S(1)}, bf16[2,144,384]{2,1,0:T(8,128)(2,1)S(1)}, bf16[2,144,384]{2,1,0:T(8,128)(2,1)S(1)}, bf16[2,144,384]{2,1,0:T(8,128)(2,1)S(1)}) custom-call(s32[32]{0:T(128)S(1)} %copy-done.7, bf16[2,2,128,768]{3,2,1,0:T(8,128)(2,1)S(1)} %pad_maximum_fusion.queries, s32[2,8,768]{2,1,0:T(8,128)S(1)} %copy-done.4, ...), custom_call_target="tpu_custom_call" | custom-call | flops 1000000 | bytes 1048576 | tf_op jit(solution)/shard_map/pallas_call | solution.py:433
  70.3 5.1 %collective-permute-done.16.refs_1_ = bf16[2,144,384]{2,1,0:T(8,128)(2,1)S(1)} collective-permute-done((bf16[2,144,384]{2,1,0:T(8,128)(2,1)S(1)}, bf16[2,144,384]{2,1,0:T(8,128)(2,1)S(1)}, u32[]{:S(2)}, u32[]{:S(2)}) %collective-permute-start.16) | collective-permute-done | bytes 221216 | tf_op jit(solution)/shard_map/ppermute | solution.py:574
  75.6 1.8 %collective-permute-done.18.refs_3_ = bf16[2,144,384]{2,1,0:T(8,128)(2,1)S(1)} collective-permute-done((bf16[2,144,384]{2,1,0:T(8,128)(2,1)S(1)}, bf16[2,144,384]{2,1,0:T(8,128)(2,1)S(1)}, u32[]{:S(2)}, u32[]{:S(2)}) %collective-permute-start.18) | collective-permute-done | bytes 221216 | tf_op jit(solution)/shard_map/ppermute | solution.py:574
  77.7 1.8 %collective-permute-start.20 = (bf16[384,256]{1,0:T(8,128)(2,1)S(1)}, bf16[384,256]{1,0:T(8,128)(2,1)S(1)}, u32[]{:S(2)}, u32[]{:S(2)}) collective-permute-start(bf16[384,256]{1,0:T(8,128)(2,1)S(1)} %shard_map.109.refs_0_), channel_id=1, source_target_pairs={{0,2},{2,4},{4,6},{6,0},{1,3},{3,5},{5,7},{7,1},{8,10},{10,12},{12... | collective-permute-start | bytes 589832 | tf_op jit(solution)/shard_map/ppermute | solution.py:577
  82.0 1.8 %collective-permute-done.20.refs_1_ = bf16[384,256]{1,0:T(8,128)(2,1)S(1)} collective-permute-done((bf16[384,256]{1,0:T(8,128)(2,1)S(1)}, bf16[384,256]{1,0:T(8,128)(2,1)S(1)}, u32[]{:S(2)}, u32[]{:S(2)}) %collective-permute-start.20) | collective-permute-done | bytes 196640 | tf_op jit(solution)/shard_map/ppermute | solution.py:577
  83.8 2.4 %collective-permute-done.21.refs_2_ = bf16[384,256]{1,0:T(8,128)(2,1)S(1)} collective-permute-done((bf16[384,256]{1,0:T(8,128)(2,1)S(1)}, bf16[384,256]{1,0:T(8,128)(2,1)S(1)}, u32[]{:S(2)}, u32[]{:S(2)}) %collective-permute-start.21) | collective-permute-done | bytes 196640 | tf_op jit(solution)/shard_map/ppermute | solution.py:577
  87.3 9.3 %collective-permute-start.23 = (bf16[384,384]{1,0:T(8,128)(2,1)S(1)}, bf16[384,384]{1,0:T(8,128)(2,1)S(1)}, u32[]{:S(2)}, u32[]{:S(2)}) collective-permute-start(bf16[384,384]{1,0:T(8,128)(2,1)S(1)} %shard_map.111), channel_id=1, source_target_pairs={{0,1},{1,0},{2,3},{3,2},{4,5},{5,4},{6,7},{7,6},{8,9},{9,8},{10,11... | collective-permute-start | bytes 884744 | tf_op jit(solution)/shard_map/ppermute | solution.py:579
  (61 shorter events, 21.0 us)
Async XLA Ops:
  6.4 16.5 %collective-permute-start.3 = (bf16[896,128]{1,0:T(8,128)(2,1)}, bf16[896,128]{1,0:T(8,128)(2,1)S(1)}, u32[]{:S(2)}, u32[]{:S(2)}) collective-permute-start(bf16[896,128]{1,0:T(8,128)(2,1)} %get-tuple-element.62), channel_id=1, source_target_pairs={{0,2},{2,4},{4,6},{6,0},{1,3},{3,5},{5,7},{7,1},{8,10},{10,12},{12... | collective-permute-start | bytes 688136 | tf_op jit(solution)/shard_map/ppermute | solution.py:536
  8.5 15.5 %collective-permute-start.4 = (bf16[896,128]{1,0:T(8,128)(2,1)}, bf16[896,128]{1,0:T(8,128)(2,1)S(1)}, u32[]{:S(2)}, u32[]{:S(2)}) collective-permute-start(bf16[896,128]{1,0:T(8,128)(2,1)} %get-tuple-element.63), channel_id=1, source_target_pairs={{0,4},{2,6},{4,0},{6,2},{1,5},{3,7},{5,1},{7,3},{8,12},{10,14},{12... | collective-permute-start | bytes 688136 | tf_op jit(solution)/shard_map/ppermute | solution.py:536
  11.0 13.0 %collective-permute-start.5 = (bf16[896,128]{1,0:T(8,128)(2,1)}, bf16[896,128]{1,0:T(8,128)(2,1)S(1)}, u32[]{:S(2)}, u32[]{:S(2)}) collective-permute-start(bf16[896,128]{1,0:T(8,128)(2,1)} %get-tuple-element.64), channel_id=1, source_target_pairs={{0,6},{2,0},{4,2},{6,4},{1,7},{3,1},{5,3},{7,5},{8,14},{10,8},{12,... | collective-permute-start | bytes 688136 | tf_op jit(solution)/shard_map/ppermute | solution.py:536
  18.9 12.6 %collective-permute-start = (bf16[2,128,384]{2,1,0:T(8,128)(2,1)S(1)}, bf16[2,128,384]{2,1,0:T(8,128)(2,1)S(1)}, u32[]{:S(2)}, u32[]{:S(2)}) collective-permute-start(bf16[2,128,384]{2,1,0:T(8,128)(2,1)S(1)} %shard_map.102), channel_id=1, source_target_pairs={{0,8},{8,16},{16,24},{24,0},{32,40},{40,48},{48,56},{56,32},{64,72... | collective-permute-start | bytes 589832 | tf_op jit(solution)/shard_map/ppermute | solution.py:540
  20.3 11.3 %collective-permute-start.1 = (bf16[2,128,384]{2,1,0:T(8,128)(2,1)S(1)}, bf16[2,128,384]{2,1,0:T(8,128)(2,1)S(1)}, u32[]{:S(2)}, u32[]{:S(2)}) collective-permute-start(bf16[2,128,384]{2,1,0:T(8,128)(2,1)S(1)} %shard_map.102), channel_id=1, source_target_pairs={{0,16},{8,24},{16,0},{24,8},{32,48},{40,56},{48,32},{56,40},{64,80... | collective-permute-start | bytes 589832 | tf_op jit(solution)/shard_map/ppermute | solution.py:540
  22.9 8.7 %collective-permute-start.2 = (bf16[2,128,384]{2,1,0:T(8,128)(2,1)S(1)}, bf16[2,128,384]{2,1,0:T(8,128)(2,1)S(1)}, u32[]{:S(2)}, u32[]{:S(2)}) collective-permute-start(bf16[2,128,384]{2,1,0:T(8,128)(2,1)S(1)} %shard_map.102), channel_id=1, source_target_pairs={{0,24},{8,0},{16,8},{24,16},{32,56},{40,32},{48,40},{56,48},{64,88... | collective-permute-start | bytes 589832 | tf_op jit(solution)/shard_map/ppermute | solution.py:540
  25.9 11.7 %collective-permute-start.7 = (bf16[2,768,128]{2,1,0:T(8,128)(2,1)S(1)}, bf16[2,768,128]{2,1,0:T(8,128)(2,1)S(1)}, u32[]{:S(2)}, u32[]{:S(2)}) collective-permute-start(bf16[2,768,128]{2,1,0:T(8,128)(2,1)S(1)} %shard_map.103.refs_0_), channel_id=1, source_target_pairs={{0,224},{8,232},{16,240},{24,248},{32,0},{40,8},{48,16},{56,24},{6... | collective-permute-start | bytes 1179656 | tf_op jit(solution)/shard_map/ppermute | solution.py:553
  31.5 9.5 %collective-permute-start.6 = (bf16[2,768,128]{2,1,0:T(8,128)(2,1)S(1)}, bf16[2,768,128]{2,1,0:T(8,128)(2,1)S(1)}, u32[]{:S(2)}, u32[]{:S(2)}) collective-permute-start(bf16[2,768,128]{2,1,0:T(8,128)(2,1)S(1)} %shard_map.103.refs_0_), channel_id=1, source_target_pairs={{0,32},{8,40},{16,48},{24,56},{32,64},{40,72},{48,80},{56,88},{64,... | collective-permute-start | bytes 1179656 | tf_op jit(solution)/shard_map/ppermute | solution.py:553
  37.6 8.8 %collective-permute-start.9 = (bf16[2,768,128]{2,1,0:T(8,128)(2,1)S(1)}, bf16[2,768,128]{2,1,0:T(8,128)(2,1)}, u32[]{:S(2)}, u32[]{:S(2)}) collective-permute-start(bf16[2,768,128]{2,1,0:T(8,128)(2,1)S(1)} %collective-permute-done.7.refs_1_), channel_id=1, source_target_pairs={{0,224},{8,232},{16,240},{24,248},{32,0},{40,8},{48,16},{56,24},{6... | collective-permute-start | bytes 1179656 | tf_op jit(solution)/shard_map/ppermute | solution.py:553
  41.0 8.6 %collective-permute-start.8 = (bf16[2,768,128]{2,1,0:T(8,128)(2,1)S(1)}, bf16[2,768,128]{2,1,0:T(8,128)(2,1)}, u32[]{:S(2)}, u32[]{:S(2)}) collective-permute-start(bf16[2,768,128]{2,1,0:T(8,128)(2,1)S(1)} %collective-permute-done.6.refs_0_), channel_id=1, source_target_pairs={{0,32},{8,40},{16,48},{24,56},{32,64},{40,72},{48,80},{56,88},{64,... | collective-permute-start | bytes 1179656 | tf_op jit(solution)/shard_map/ppermute | solution.py:553
  42.5 8.4 %collective-permute-start.10 = (bf16[256,768]{1,0:T(8,128)(2,1)S(1)}, bf16[256,768]{1,0:T(8,128)(2,1)S(1)}, u32[]{:S(2)}, u32[]{:S(2)}) collective-permute-start(bf16[256,768]{1,0:T(8,128)(2,1)S(1)} %get-tuple-element.98), channel_id=1, source_target_pairs={{0,2},{2,4},{4,6},{6,0},{1,3},{3,5},{5,7},{7,1},{8,10},{10,12},{12... | collective-permute-start | bytes 1179656 | tf_op jit(solution)/shard_map/ppermute | solution.py:550
  46.4 9.2 %collective-permute-start.13 = (bf16[2,768,128]{2,1,0:T(8,128)(2,1)}, bf16[2,768,128]{2,1,0:T(8,128)(2,1)S(1)}, u32[]{:S(2)}, u32[]{:S(2)}) collective-permute-start(bf16[2,768,128]{2,1,0:T(8,128)(2,1)} %collective-permute-done.9.refs_1_), channel_id=1, source_target_pairs={{0,224},{8,232},{16,240},{24,248},{32,0},{40,8},{48,16},{56,24},{6... | collective-permute-start | bytes 1179656 | tf_op jit(solution)/shard_map/ppermute | solution.py:553
  49.7 8.0 %collective-permute-start.11 = (bf16[2,768,128]{2,1,0:T(8,128)(2,1)}, bf16[2,768,128]{2,1,0:T(8,128)(2,1)S(1)}, u32[]{:S(2)}, u32[]{:S(2)}) collective-permute-start(bf16[2,768,128]{2,1,0:T(8,128)(2,1)} %collective-permute-done.8.refs_0_), channel_id=1, source_target_pairs={{0,32},{8,40},{16,48},{24,56},{32,64},{40,72},{48,80},{56,88},{64,... | collective-permute-start | bytes 1179656 | tf_op jit(solution)/shard_map/ppermute | solution.py:553
  49.7 9.9 %collective-permute-start.15 = (bf16[256,768]{1,0:T(8,128)(2,1)S(1)}, bf16[256,768]{1,0:T(8,128)(2,1)S(1)}, u32[]{:S(2)}, u32[]{:S(2)}) collective-permute-start(bf16[256,768]{1,0:T(8,128)(2,1)S(1)} %get-tuple-element.97), channel_id=1, source_target_pairs={{0,6},{2,0},{4,2},{6,4},{1,7},{3,1},{5,3},{7,5},{8,14},{10,8},{12,... | collective-permute-start | bytes 1179656 | tf_op jit(solution)/shard_map/ppermute | solution.py:550
  57.7 5.4 %collective-permute-start.14 = (bf16[768,128]{1,0:T(8,128)(2,1)S(1)}, bf16[768,128]{1,0:T(8,128)(2,1)S(1)}, u32[]{:S(2)}, u32[]{:S(2)}) collective-permute-start(bf16[768,128]{1,0:T(8,128)(2,1)S(1)} %slice_bitcast_fusion), channel_id=1, source_target_pairs={{0,224},{8,232},{16,240},{24,248},{32,0},{40,8},{48,16},{56,24},{6... | collective-permute-start | bytes 589832 | tf_op jit(solution)/shard_map/ppermute | solution.py:553
  57.8 6.9 %collective-permute-start.12 = (bf16[768,128]{1,0:T(8,128)(2,1)S(1)}, bf16[768,128]{1,0:T(8,128)(2,1)S(1)}, u32[]{:S(2)}, u32[]{:S(2)}) collective-permute-start(bf16[768,128]{1,0:T(8,128)(2,1)S(1)} %slice_bitcast_fusion.1), channel_id=1, source_target_pairs={{0,32},{8,40},{16,48},{24,56},{32,64},{40,72},{48,80},{56,88},{64,... | collective-permute-start | bytes 589832 | tf_op jit(solution)/shard_map/ppermute | solution.py:553
  59.4 10.9 %collective-permute-start.19 = (bf16[256,768]{1,0:T(8,128)(2,1)S(1)}, bf16[256,768]{1,0:T(8,128)(2,1)S(1)}, u32[]{:S(2)}, u32[]{:S(2)}) collective-permute-start(bf16[256,768]{1,0:T(8,128)(2,1)S(1)} %get-tuple-element.96), channel_id=1, source_target_pairs={{0,4},{2,6},{4,0},{6,2},{1,5},{3,7},{5,1},{7,3},{8,12},{10,14},{12... | collective-permute-start | bytes 1179656 | tf_op jit(solution)/shard_map/ppermute | solution.py:550
  68.6 6.7 %collective-permute-start.16 = (bf16[2,144,384]{2,1,0:T(8,128)(2,1)S(1)}, bf16[2,144,384]{2,1,0:T(8,128)(2,1)S(1)}, u32[]{:S(2)}, u32[]{:S(2)}) collective-permute-start(bf16[2,144,384]{2,1,0:T(8,128)(2,1)S(1)} %get-tuple-element.85), channel_id=1, source_target_pairs={{0,16},{8,24},{16,0},{24,8},{32,48},{40,56},{48,32},{56,40},{64,80... | collective-permute-start | bytes 663560 | tf_op jit(solution)/shard_map/ppermute | solution.py:574
  68.7 6.9 %collective-permute-start.17 = (bf16[2,144,384]{2,1,0:T(8,128)(2,1)S(1)}, bf16[2,144,384]{2,1,0:T(8,128)(2,1)S(1)}, u32[]{:S(2)}, u32[]{:S(2)}) collective-permute-start(bf16[2,144,384]{2,1,0:T(8,128)(2,1)S(1)} %get-tuple-element.86), channel_id=1, source_target_pairs={{0,24},{8,0},{16,8},{24,16},{32,56},{40,32},{48,40},{56,48},{64,88... | collective-permute-start | bytes 663560 | tf_op jit(solution)/shard_map/ppermute | solution.py:574
  69.4 8.0 %collective-permute-start.18 = (bf16[2,144,384]{2,1,0:T(8,128)(2,1)S(1)}, bf16[2,144,384]{2,1,0:T(8,128)(2,1)S(1)}, u32[]{:S(2)}, u32[]{:S(2)}) collective-permute-start(bf16[2,144,384]{2,1,0:T(8,128)(2,1)S(1)} %get-tuple-element.87), channel_id=1, source_target_pairs={{0,8},{8,16},{16,24},{24,0},{32,40},{40,48},{48,56},{56,32},{64,72... | collective-permute-start | bytes 663560 | tf_op jit(solution)/shard_map/ppermute | solution.py:574
  77.7 6.1 %collective-permute-start.20 = (bf16[384,256]{1,0:T(8,128)(2,1)S(1)}, bf16[384,256]{1,0:T(8,128)(2,1)S(1)}, u32[]{:S(2)}, u32[]{:S(2)}) collective-permute-start(bf16[384,256]{1,0:T(8,128)(2,1)S(1)} %shard_map.109.refs_0_), channel_id=1, source_target_pairs={{0,2},{2,4},{4,6},{6,0},{1,3},{3,5},{5,7},{7,1},{8,10},{10,12},{12... | collective-permute-start | bytes 589832 | tf_op jit(solution)/shard_map/ppermute | solution.py:577
  79.5 6.7 %collective-permute-start.21 = (bf16[384,256]{1,0:T(8,128)(2,1)S(1)}, bf16[384,256]{1,0:T(8,128)(2,1)S(1)}, u32[]{:S(2)}, u32[]{:S(2)}) collective-permute-start(bf16[384,256]{1,0:T(8,128)(2,1)S(1)} %shard_map.109.refs_0_), channel_id=1, source_target_pairs={{0,4},{2,6},{4,0},{6,2},{1,5},{3,7},{5,1},{7,3},{8,12},{10,14},{12... | collective-permute-start | bytes 589832 | tf_op jit(solution)/shard_map/ppermute | solution.py:577
  81.0 5.2 %collective-permute-start.22 = (bf16[384,256]{1,0:T(8,128)(2,1)S(1)}, bf16[384,256]{1,0:T(8,128)(2,1)S(1)}, u32[]{:S(2)}, u32[]{:S(2)}) collective-permute-start(bf16[384,256]{1,0:T(8,128)(2,1)S(1)} %shard_map.109.refs_0_), channel_id=1, source_target_pairs={{0,6},{2,0},{4,2},{6,4},{1,7},{3,1},{5,3},{7,5},{8,14},{10,8},{12,... | collective-permute-start | bytes 589832 | tf_op jit(solution)/shard_map/ppermute | solution.py:577
  87.3 10.6 %collective-permute-start.23 = (bf16[384,384]{1,0:T(8,128)(2,1)S(1)}, bf16[384,384]{1,0:T(8,128)(2,1)S(1)}, u32[]{:S(2)}, u32[]{:S(2)}) collective-permute-start(bf16[384,384]{1,0:T(8,128)(2,1)S(1)} %shard_map.111), channel_id=1, source_target_pairs={{0,1},{1,0},{2,3},{3,2},{4,5},{5,4},{6,7},{7,6},{8,9},{9,8},{10,11... | collective-permute-start | bytes 884744 | tf_op jit(solution)/shard_map/ppermute | solution.py:579
  (8 other events, 41.0 us)

commit v2 on v1

--- a/solution.py
+++ b/solution.py
@@ -21,7 +21,7 @@
 QUERY_SCALE = HEAD ** (-0.5) * math.log2(math.e)
 
 
-CHUNKS = 6
+CHUNKS = 2
 ATTEND_FLOPS = 10**6
 
 
@@ -562,12 +562,12 @@
     right_2 = lax.optimization_barrier((state[0], right_2))[1]
     left_2 = lax.optimization_barrier((state[0], left_2))[1]
     right_3, left_3 = ring(right_2, left_2)
-    state, weights[1] = lax.optimization_barrier((state, weights[1]))
+    info, weights[1] = lax.optimization_barrier((info, weights[1]))
     state = attend(info, queries, spans, {2: (right_2,), SEQ_Z - 2: (left_2,)}, state)
     right_3 = lax.optimization_barrier((state[0], right_3))[1]
     left_3 = lax.optimization_barrier((state[0], left_3))[1]
     far = ring(right_3[0], left_3[1])
-    state, weights[3] = lax.optimization_barrier((state, weights[3]))
+    info, weights[3] = lax.optimization_barrier((info, weights[3]))
     state = attend(info, queries, spans, {3: (right_3,), SEQ_Z - 3: (left_3,)}, state)
     parts = attend(info, queries, spans, {half: far}, state, last=True)
 

time: 98.6 us -> 97 us (0.984)
  Pallas kernels: 32.3 us -> 22.3 us
  waiting for transfers between devices: 17.7 us -> 23.7 us
  starting transfers between devices: 41.5 us -> 43.5 us
    pallas_call x5, Pallas kernels: 19.2 us -> 9.42 us  [attend(): pl.pallas_call(functools.partial(attend_kernel, first, last, tuple(blocks...]
    ppermute x3, starting transfers between devices: 1.64 us -> 6.57 us  [per_device(): lax.ppermute(parts[g], 'seq', around_y(-g))]
    ppermute x1, starting transfers between devices: 9.35 us -> 5.08 us  [per_device(): theirs = lax.ppermute(theirs, 'mp', [(0, 1), (1, 0)])]
    ppermute x4, waiting for transfers between devices: 2.28 us -> 6.07 us  [ring(): lax.ppermute(left, 'seq', around_z(-1))]
    ppermute x3, starting transfers between devices: 1.52 us -> 3.24 us  [per_device(): lax.ppermute(columns(s), 'cache', around_x(s))]
    ppermute x4, waiting for transfers between devices: 3.68 us -> 5.3 us  [ring(): lax.ppermute(right, 'seq', around_z(1))]
    ppermute x4, starting transfers between devices: 12.4 us -> 13.9 us  [ring(): lax.ppermute(left, 'seq', around_z(-1))]
    ppermute x4, starting transfers between devices: 1.53 us -> 0.28 us  [ring(): lax.ppermute(right, 'seq', around_z(1))]
  transfers between devices with their start and end apart: 24 -> 24, of which waited for: 10 -> 12; matrix products, arithmetic and copies ran while one was open for 2% -> 2% of each run, Pallas kernels for 26% -> 17%
where the time goes in v2:
time: 97 us; the launch traced here: 96.7 us
  starting transfers between devices  43.5 us (45%)
  waiting for transfers between devices  23.7 us (24%)
  Pallas kernels  22.3 us (23%)
  local copies, waits for them, and re-layouts  4.59 us (5%)
  other arithmetic  2.34 us (2%)
    ppermute x4, starting transfers between devices, ring(): lax.ppermute(left, 'seq', around_z(-1))  13.9 us
    pallas_call x5, Pallas kernels, attend(): pl.pallas_call(functools.partial(attend_kernel, first, last, tuple(blocks...  9.42 us
    ppermute x3, waiting for transfers between devices, per_device(): lax.ppermute(parts[g], 'seq', around_y(-g))  6.99 us
    ppermute x3, starting transfers between devices, per_device(): lax.ppermute(parts[g], 'seq', around_y(-g))  6.57 us
    ppermute x4, waiting for transfers between devices, ring(): lax.ppermute(left, 'seq', around_z(-1))  6.07 us
    ppermute x3, starting transfers between devices, per_device(): lax.ppermute(messages[s], 'cache', around_x(s))  5.72 us
    ppermute x4, waiting for transfers between devices, ring(): lax.ppermute(right, 'seq', around_z(1))  5.3 us
    ppermute x3, waiting for transfers between devices, per_device(): lax.ppermute(attended, 'cache', around_x(s))  5.26 us
  transfers between devices with their start and end apart: 24, of which 12 were waited for; matrix products, arithmetic and copies ran while one was open for 2% of the time, Pallas kernels for 17%

profile of v2, /device:TPU:1, one launch (start us, length us, event | category | flops | bytes accessed | tf_op | source)
XLA Modules:
  0.0 96.7 jit_solution(780809208005298984)
XLA Ops:
  1.4 4.8 %shard_map.100 = (bf16[896,128]{1,0:T(8,128)(2,1)}, bf16[896,128]{1,0:T(8,128)(2,1)}, bf16[896,128]{1,0:T(8,128)(2,1)}, bf16[896,128]{1,0:T(8,128)(2,1)}, s32[2,8,768]{2,1,0:T(8,128)}, /*index=5*/s32[32]{0:T(128)}) custom-call(s32[43]{0:T(128)} %pad_add_fusion.1.where, bf16[384,3072]{1,0:T(8,128)(2,1)} %tokens.3, bf16[2,3072,128]{2,1,0:T(8,128)(2,1)} %down.1, ...), custom_call_target="tpu_custom_call" | custom-call | flops 600000000 | bytes 6291456 | tf_op jit(solution)/shard_map/pallas_call | solution.py:158
  6.3 2.1 %collective-permute-start = (bf16[896,128]{1,0:T(8,128)(2,1)}, bf16[896,128]{1,0:T(8,128)(2,1)S(1)}, u32[]{:S(2)}, u32[]{:S(2)}) collective-permute-start(bf16[896,128]{1,0:T(8,128)(2,1)} %get-tuple-element.58), channel_id=1, source_target_pairs={{0,2},{2,4},{4,6},{6,0},{1,3},{3,5},{5,7},{7,1},{8,10},{10,12},{12... | collective-permute-start | bytes 688136 | tf_op jit(solution)/shard_map/ppermute | solution.py:536
  8.4 2.5 %collective-permute-start.1 = (bf16[896,128]{1,0:T(8,128)(2,1)}, bf16[896,128]{1,0:T(8,128)(2,1)S(1)}, u32[]{:S(2)}, u32[]{:S(2)}) collective-permute-start(bf16[896,128]{1,0:T(8,128)(2,1)} %get-tuple-element.59), channel_id=1, source_target_pairs={{0,4},{2,6},{4,0},{6,2},{1,5},{3,7},{5,1},{7,3},{8,12},{10,14},{12... | collective-permute-start | bytes 688136 | tf_op jit(solution)/shard_map/ppermute | solution.py:536
  15.1 2.1 %shard_map.101 = (f32[384,256]{1,0:T(8,128)S(1)}, f32[384,256]{1,0:T(8,128)S(1)}) custom-call(bf16[384,3072]{1,0:T(8,128)(2,1)S(1)} %copy-done, bf16[3072,256]{1,0:T(8,128)(2,1)S(1)} %copy-done.1, bf16[3072,256]{1,0:T(8,128)(2,1)S(1)} %copy-done.2), custom_call_target="tpu_custom_call" | custom-call | flops 1200000000 | bytes 6291456 | tf_op jit(solution)/shard_map/pallas_call | solution.py:245
  20.1 2.6 %collective-permute-start.6 = (bf16[2,128,384]{2,1,0:T(8,128)(2,1)S(1)}, bf16[2,128,384]{2,1,0:T(8,128)(2,1)S(1)}, u32[]{:S(2)}, u32[]{:S(2)}) collective-permute-start(bf16[2,128,384]{2,1,0:T(8,128)(2,1)S(1)} %shard_map.103), channel_id=1, source_target_pairs={{0,16},{8,24},{16,0},{24,8},{32,48},{40,56},{48,32},{56,40},{64,80... | collective-permute-start | bytes 589832 | tf_op jit(solution)/shard_map/ppermute | solution.py:540
  23.9 1.8 %shard_map.102.refs_0_ = bf16[2,768,128]{2,1,0:T(8,128)(2,1)S(1)} custom-call(s32[43]{0:T(128)S(1)} %copy-done.6, f32[384,256]{1,0:T(8,128)S(1)} %get-tuple-element.55.key, f32[384,256]{1,0:T(8,128)S(1)} %get-tuple-element.56.value, bf16[896,128]{1,0:T(8,128)(2,1)S(1)} %copy-done.5, bf16[896,128]{1,0:T(8,128)(2,1)S(1)} %collective-permute-done.refs_1_, ...), custom_call_target="tpu_custom_call" | custom-call | flops 400000000 | bytes 2097152 | tf_op jit(solution)/shard_map/pallas_call | solution.py:288
  25.7 5.7 %collective-permute-start.9 = (bf16[2,768,128]{2,1,0:T(8,128)(2,1)S(1)}, bf16[2,768,128]{2,1,0:T(8,128)(2,1)S(1)}, u32[]{:S(2)}, u32[]{:S(2)}) collective-permute-start(bf16[2,768,128]{2,1,0:T(8,128)(2,1)S(1)} %shard_map.102.refs_0_), channel_id=1, source_target_pairs={{0,224},{8,232},{16,240},{24,248},{32,0},{40,8},{48,16},{56,24},{6... | collective-permute-start | bytes 1179656 | tf_op jit(solution)/shard_map/ppermute | solution.py:553
  31.6 3.6 %shard_map.104 = (f32[2,2,128,768]{3,2,1,0:T(8,128)S(1)}, f32[2,2,8,768]{3,2,1,0:T(8,128)S(1)}) custom-call(s32[32]{0:T(128)S(1)} %copy-done.7, bf16[2,2,128,768]{3,2,1,0:T(8,128)(2,1)S(1)} %pad_maximum_fusion.queries, s32[2,8,768]{2,1,0:T(8,128)S(1)} %copy-done.4, bf16[2,768,128]{2,1,0:T(8,128)(2,1)S(1)} %shard_map.102.refs_0_), custom_call_target="tpu_custom_call" | custom-call | flops 1000000 | bytes 1048576 | tf_op jit(solution)/shard_map/pallas_call | solution.py:433
  35.2 2.3 %collective-permute-done.9.refs_1_ = bf16[2,768,128]{2,1,0:T(8,128)(2,1)S(1)} collective-permute-done((bf16[2,768,128]{2,1,0:T(8,128)(2,1)S(1)}, bf16[2,768,128]{2,1,0:T(8,128)(2,1)S(1)}, u32[]{:S(2)}, u32[]{:S(2)}) %collective-permute-start.9) | collective-permute-done | bytes 393248 | tf_op jit(solution)/shard_map/ppermute | solution.py:553
  37.4 3.4 %collective-permute-start.11 = (bf16[2,768,128]{2,1,0:T(8,128)(2,1)S(1)}, bf16[2,768,128]{2,1,0:T(8,128)(2,1)}, u32[]{:S(2)}, u32[]{:S(2)}) collective-permute-start(bf16[2,768,128]{2,1,0:T(8,128)(2,1)S(1)} %collective-permute-done.9.refs_1_), channel_id=1, source_target_pairs={{0,224},{8,232},{16,240},{24,248},{32,0},{40,8},{48,16},{56,24},{6... | collective-permute-start | bytes 1179656 | tf_op jit(solution)/shard_map/ppermute | solution.py:553
  42.7 2.2 %shard_map.105 = (f32[2,2,128,768]{3,2,1,0:T(8,128)S(1)}, f32[2,2,8,768]{3,2,1,0:T(8,128)S(1)}) custom-call(s32[32]{0:T(128)S(1)} %copy-done.7, bf16[2,2,128,768]{3,2,1,0:T(8,128)(2,1)S(1)} %pad_maximum_fusion.queries, s32[2,8,768]{2,1,0:T(8,128)S(1)} %copy-done.4, bf16[2,768,128]{2,1,0:T(8,128)(2,1)S(1)} %collective-permute-done.8.refs_0_, ...), custom_call_target="tpu_custom_call" | custom-call | flops 2000000 | bytes 1048576 | tf_op jit(solution)/shard_map/pallas_call | solution.py:433
  46.0 3.5 %collective-permute-start.14 = (bf16[2,768,128]{2,1,0:T(8,128)(2,1)}, bf16[2,768,128]{2,1,0:T(8,128)(2,1)S(1)}, u32[]{:S(2)}, u32[]{:S(2)}) collective-permute-start(bf16[2,768,128]{2,1,0:T(8,128)(2,1)} %collective-permute-done.11.refs_1_), channel_id=1, source_target_pairs={{0,224},{8,232},{16,240},{24,248},{32,0},{40,8},{48,16},{56,24},{6... | collective-permute-start | bytes 1179656 | tf_op jit(solution)/shard_map/ppermute | solution.py:553
  49.5 1.9 %collective-permute-start.4 = (bf16[256,768]{1,0:T(8,128)(2,1)S(1)}, bf16[256,768]{1,0:T(8,128)(2,1)S(1)}, u32[]{:S(2)}, u32[]{:S(2)}) collective-permute-start(bf16[256,768]{1,0:T(8,128)(2,1)S(1)} %get-tuple-element.93), channel_id=1, source_target_pairs={{0,6},{2,0},{4,2},{6,4},{1,7},{3,1},{5,3},{7,5},{8,14},{10,8},{12,... | collective-permute-start | bytes 1179656 | tf_op jit(solution)/shard_map/ppermute | solution.py:550
  51.4 1.9 %shard_map.106 = (f32[2,2,128,768]{3,2,1,0:T(8,128)S(1)}, f32[2,2,8,768]{3,2,1,0:T(8,128)S(1)}) custom-call(s32[32]{0:T(128)S(1)} %copy-done.7, bf16[2,2,128,768]{3,2,1,0:T(8,128)(2,1)S(1)} %pad_maximum_fusion.queries, s32[2,8,768]{2,1,0:T(8,128)S(1)} %copy-done.4, bf16[2,768,128]{2,1,0:T(8,128)(2,1)} %collective-permute-done.10.refs_0_, ...), custom_call_target="tpu_custom_call" | custom-call | flops 2000000 | bytes 1048576 | tf_op jit(solution)/shard_map/pallas_call | solution.py:433
  54.5 3.0 %collective-permute-done.12.refs_0_ = bf16[2,768,128]{2,1,0:T(8,128)(2,1)S(1)} collective-permute-done((bf16[2,768,128]{2,1,0:T(8,128)(2,1)}, bf16[2,768,128]{2,1,0:T(8,128)(2,1)S(1)}, u32[]{:S(2)}, u32[]{:S(2)}) %collective-permute-start.12) | collective-permute-done | bytes 393248 | tf_op jit(solution)/shard_map/ppermute | solution.py:553
  62.5 2.3 %collective-permute-done.13.refs_0_ = bf16[768,128]{1,0:T(8,128)(2,1)S(1)} collective-permute-done((bf16[768,128]{1,0:T(8,128)(2,1)S(1)}, bf16[768,128]{1,0:T(8,128)(2,1)S(1)}, u32[]{:S(2)}, u32[]{:S(2)}) %collective-permute-start.13) | collective-permute-done | bytes 196640 | tf_op jit(solution)/shard_map/ppermute | solution.py:553
  65.7 5.1 %collective-permute-start.16 = (bf16[2,144,384]{2,1,0:T(8,128)(2,1)S(1)}, bf16[2,144,384]{2,1,0:T(8,128)(2,1)S(1)}, u32[]{:S(2)}, u32[]{:S(2)}) collective-permute-start(bf16[2,144,384]{2,1,0:T(8,128)(2,1)S(1)} %get-tuple-element.81), channel_id=1, source_target_pairs={{0,16},{8,24},{16,0},{24,8},{32,48},{40,56},{48,32},{56,40},{64,80... | collective-permute-start | bytes 663560 | tf_op jit(solution)/shard_map/ppermute | solution.py:574
  72.3 2.0 %collective-permute-done.16.refs_1_ = bf16[2,144,384]{2,1,0:T(8,128)(2,1)S(1)} collective-permute-done((bf16[2,144,384]{2,1,0:T(8,128)(2,1)S(1)}, bf16[2,144,384]{2,1,0:T(8,128)(2,1)S(1)}, u32[]{:S(2)}, u32[]{:S(2)}) %collective-permute-start.16) | collective-permute-done | bytes 221216 | tf_op jit(solution)/shard_map/ppermute | solution.py:574
  74.3 3.0 %collective-permute-done.17.refs_2_ = bf16[2,144,384]{2,1,0:T(8,128)(2,1)S(1)} collective-permute-done((bf16[2,144,384]{2,1,0:T(8,128)(2,1)S(1)}, bf16[2,144,384]{2,1,0:T(8,128)(2,1)S(1)}, u32[]{:S(2)}, u32[]{:S(2)}) %collective-permute-start.17) | collective-permute-done | bytes 221216 | tf_op jit(solution)/shard_map/ppermute | solution.py:574
  77.3 2.0 %collective-permute-done.18.refs_3_ = bf16[2,144,384]{2,1,0:T(8,128)(2,1)S(1)} collective-permute-done((bf16[2,144,384]{2,1,0:T(8,128)(2,1)S(1)}, bf16[2,144,384]{2,1,0:T(8,128)(2,1)S(1)}, u32[]{:S(2)}, u32[]{:S(2)}) %collective-permute-start.18) | collective-permute-done | bytes 221216 | tf_op jit(solution)/shard_map/ppermute | solution.py:574
  79.7 3.5 %collective-permute-start.21 = (bf16[384,256]{1,0:T(8,128)(2,1)S(1)}, bf16[384,256]{1,0:T(8,128)(2,1)S(1)}, u32[]{:S(2)}, u32[]{:S(2)}) collective-permute-start(bf16[384,256]{1,0:T(8,128)(2,1)S(1)} %shard_map.109.refs_0_), channel_id=1, source_target_pairs={{0,4},{2,6},{4,0},{6,2},{1,5},{3,7},{5,1},{7,3},{8,12},{10,14},{12... | collective-permute-start | bytes 589832 | tf_op jit(solution)/shard_map/ppermute | solution.py:577
  83.2 2.2 %collective-permute-done.20.refs_1_ = bf16[384,256]{1,0:T(8,128)(2,1)S(1)} collective-permute-done((bf16[384,256]{1,0:T(8,128)(2,1)S(1)}, bf16[384,256]{1,0:T(8,128)(2,1)S(1)}, u32[]{:S(2)}, u32[]{:S(2)}) %collective-permute-start.20) | collective-permute-done | bytes 196640 | tf_op jit(solution)/shard_map/ppermute | solution.py:577
  85.4 3.1 %collective-permute-done.21.refs_2_ = bf16[384,256]{1,0:T(8,128)(2,1)S(1)} collective-permute-done((bf16[384,256]{1,0:T(8,128)(2,1)S(1)}, bf16[384,256]{1,0:T(8,128)(2,1)S(1)}, u32[]{:S(2)}, u32[]{:S(2)}) %collective-permute-start.21) | collective-permute-done | bytes 196640 | tf_op jit(solution)/shard_map/ppermute | solution.py:577
  89.6 5.1 %collective-permute-start.23 = (bf16[384,384]{1,0:T(8,128)(2,1)S(1)}, bf16[384,384]{1,0:T(8,128)(2,1)S(1)}, u32[]{:S(2)}, u32[]{:S(2)}) collective-permute-start(bf16[384,384]{1,0:T(8,128)(2,1)S(1)} %shard_map.111), channel_id=1, source_target_pairs={{0,1},{1,0},{2,3},{3,2},{4,5},{5,4},{6,7},{7,6},{8,9},{9,8},{10,11... | collective-permute-start | bytes 884744 | tf_op jit(solution)/shard_map/ppermute | solution.py:579
  (61 shorter events, 24.9 us)
Async XLA Ops:
  6.3 16.5 %collective-permute-start = (bf16[896,128]{1,0:T(8,128)(2,1)}, bf16[896,128]{1,0:T(8,128)(2,1)S(1)}, u32[]{:S(2)}, u32[]{:S(2)}) collective-permute-start(bf16[896,128]{1,0:T(8,128)(2,1)} %get-tuple-element.58), channel_id=1, source_target_pairs={{0,2},{2,4},{4,6},{6,0},{1,3},{3,5},{5,7},{7,1},{8,10},{10,12},{12... | collective-permute-start | bytes 688136 | tf_op jit(solution)/shard_map/ppermute | solution.py:536
  8.4 15.5 %collective-permute-start.1 = (bf16[896,128]{1,0:T(8,128)(2,1)}, bf16[896,128]{1,0:T(8,128)(2,1)S(1)}, u32[]{:S(2)}, u32[]{:S(2)}) collective-permute-start(bf16[896,128]{1,0:T(8,128)(2,1)} %get-tuple-element.59), channel_id=1, source_target_pairs={{0,4},{2,6},{4,0},{6,2},{1,5},{3,7},{5,1},{7,3},{8,12},{10,14},{12... | collective-permute-start | bytes 688136 | tf_op jit(solution)/shard_map/ppermute | solution.py:536
  10.8 13.0 %collective-permute-start.2 = (bf16[896,128]{1,0:T(8,128)(2,1)}, bf16[896,128]{1,0:T(8,128)(2,1)S(1)}, u32[]{:S(2)}, u32[]{:S(2)}) collective-permute-start(bf16[896,128]{1,0:T(8,128)(2,1)} %get-tuple-element.60), channel_id=1, source_target_pairs={{0,6},{2,0},{4,2},{6,4},{1,7},{3,1},{5,3},{7,5},{8,14},{10,8},{12,... | collective-permute-start | bytes 688136 | tf_op jit(solution)/shard_map/ppermute | solution.py:536
  18.8 12.6 %collective-permute-start.5 = (bf16[2,128,384]{2,1,0:T(8,128)(2,1)S(1)}, bf16[2,128,384]{2,1,0:T(8,128)(2,1)S(1)}, u32[]{:S(2)}, u32[]{:S(2)}) collective-permute-start(bf16[2,128,384]{2,1,0:T(8,128)(2,1)S(1)} %shard_map.103), channel_id=1, source_target_pairs={{0,8},{8,16},{16,24},{24,0},{32,40},{40,48},{48,56},{56,32},{64,72... | collective-permute-start | bytes 589832 | tf_op jit(solution)/shard_map/ppermute | solution.py:540
  20.1 11.3 %collective-permute-start.6 = (bf16[2,128,384]{2,1,0:T(8,128)(2,1)S(1)}, bf16[2,128,384]{2,1,0:T(8,128)(2,1)S(1)}, u32[]{:S(2)}, u32[]{:S(2)}) collective-permute-start(bf16[2,128,384]{2,1,0:T(8,128)(2,1)S(1)} %shard_map.103), channel_id=1, source_target_pairs={{0,16},{8,24},{16,0},{24,8},{32,48},{40,56},{48,32},{56,40},{64,80... | collective-permute-start | bytes 589832 | tf_op jit(solution)/shard_map/ppermute | solution.py:540
  22.8 8.7 %collective-permute-start.7 = (bf16[2,128,384]{2,1,0:T(8,128)(2,1)S(1)}, bf16[2,128,384]{2,1,0:T(8,128)(2,1)S(1)}, u32[]{:S(2)}, u32[]{:S(2)}) collective-permute-start(bf16[2,128,384]{2,1,0:T(8,128)(2,1)S(1)} %shard_map.103), channel_id=1, source_target_pairs={{0,24},{8,0},{16,8},{24,16},{32,56},{40,32},{48,40},{56,48},{64,88... | collective-permute-start | bytes 589832 | tf_op jit(solution)/shard_map/ppermute | solution.py:540
  25.7 11.7 %collective-permute-start.9 = (bf16[2,768,128]{2,1,0:T(8,128)(2,1)S(1)}, bf16[2,768,128]{2,1,0:T(8,128)(2,1)S(1)}, u32[]{:S(2)}, u32[]{:S(2)}) collective-permute-start(bf16[2,768,128]{2,1,0:T(8,128)(2,1)S(1)} %shard_map.102.refs_0_), channel_id=1, source_target_pairs={{0,224},{8,232},{16,240},{24,248},{32,0},{40,8},{48,16},{56,24},{6... | collective-permute-start | bytes 1179656 | tf_op jit(solution)/shard_map/ppermute | solution.py:553
  31.4 9.5 %collective-permute-start.8 = (bf16[2,768,128]{2,1,0:T(8,128)(2,1)S(1)}, bf16[2,768,128]{2,1,0:T(8,128)(2,1)S(1)}, u32[]{:S(2)}, u32[]{:S(2)}) collective-permute-start(bf16[2,768,128]{2,1,0:T(8,128)(2,1)S(1)} %shard_map.102.refs_0_), channel_id=1, source_target_pairs={{0,32},{8,40},{16,48},{24,56},{32,64},{40,72},{48,80},{56,88},{64,... | collective-permute-start | bytes 1179656 | tf_op jit(solution)/shard_map/ppermute | solution.py:553
  37.4 8.5 %collective-permute-start.11 = (bf16[2,768,128]{2,1,0:T(8,128)(2,1)S(1)}, bf16[2,768,128]{2,1,0:T(8,128)(2,1)}, u32[]{:S(2)}, u32[]{:S(2)}) collective-permute-start(bf16[2,768,128]{2,1,0:T(8,128)(2,1)S(1)} %collective-permute-done.9.refs_1_), channel_id=1, source_target_pairs={{0,224},{8,232},{16,240},{24,248},{32,0},{40,8},{48,16},{56,24},{6... | collective-permute-start | bytes 1179656 | tf_op jit(solution)/shard_map/ppermute | solution.py:553
  40.9 8.6 %collective-permute-start.10 = (bf16[2,768,128]{2,1,0:T(8,128)(2,1)S(1)}, bf16[2,768,128]{2,1,0:T(8,128)(2,1)}, u32[]{:S(2)}, u32[]{:S(2)}) collective-permute-start(bf16[2,768,128]{2,1,0:T(8,128)(2,1)S(1)} %collective-permute-done.8.refs_0_), channel_id=1, source_target_pairs={{0,32},{8,40},{16,48},{24,56},{32,64},{40,72},{48,80},{56,88},{64,... | collective-permute-start | bytes 1179656 | tf_op jit(solution)/shard_map/ppermute | solution.py:553
  42.3 9.1 %collective-permute-start.3 = (bf16[256,768]{1,0:T(8,128)(2,1)S(1)}, bf16[256,768]{1,0:T(8,128)(2,1)S(1)}, u32[]{:S(2)}, u32[]{:S(2)}) collective-permute-start(bf16[256,768]{1,0:T(8,128)(2,1)S(1)} %get-tuple-element.94), channel_id=1, source_target_pairs={{0,2},{2,4},{4,6},{6,0},{1,3},{3,5},{5,7},{7,1},{8,10},{10,12},{12... | collective-permute-start | bytes 1179656 | tf_op jit(solution)/shard_map/ppermute | solution.py:550
  46.0 8.6 %collective-permute-start.14 = (bf16[2,768,128]{2,1,0:T(8,128)(2,1)}, bf16[2,768,128]{2,1,0:T(8,128)(2,1)S(1)}, u32[]{:S(2)}, u32[]{:S(2)}) collective-permute-start(bf16[2,768,128]{2,1,0:T(8,128)(2,1)} %collective-permute-done.11.refs_1_), channel_id=1, source_target_pairs={{0,224},{8,232},{16,240},{24,248},{32,0},{40,8},{48,16},{56,24},{6... | collective-permute-start | bytes 1179656 | tf_op jit(solution)/shard_map/ppermute | solution.py:553
  49.5 8.0 %collective-permute-start.12 = (bf16[2,768,128]{2,1,0:T(8,128)(2,1)}, bf16[2,768,128]{2,1,0:T(8,128)(2,1)S(1)}, u32[]{:S(2)}, u32[]{:S(2)}) collective-permute-start(bf16[2,768,128]{2,1,0:T(8,128)(2,1)} %collective-permute-done.10.refs_0_), channel_id=1, source_target_pairs={{0,32},{8,40},{16,48},{24,56},{32,64},{40,72},{48,80},{56,88},{64,... | collective-permute-start | bytes 1179656 | tf_op jit(solution)/shard_map/ppermute | solution.py:553
  49.5 10.6 %collective-permute-start.4 = (bf16[256,768]{1,0:T(8,128)(2,1)S(1)}, bf16[256,768]{1,0:T(8,128)(2,1)S(1)}, u32[]{:S(2)}, u32[]{:S(2)}) collective-permute-start(bf16[256,768]{1,0:T(8,128)(2,1)S(1)} %get-tuple-element.93), channel_id=1, source_target_pairs={{0,6},{2,0},{4,2},{6,4},{1,7},{3,1},{5,3},{7,5},{8,14},{10,8},{12,... | collective-permute-start | bytes 1179656 | tf_op jit(solution)/shard_map/ppermute | solution.py:550
  57.6 4.9 %collective-permute-start.15 = (bf16[768,128]{1,0:T(8,128)(2,1)S(1)}, bf16[768,128]{1,0:T(8,128)(2,1)S(1)}, u32[]{:S(2)}, u32[]{:S(2)}) collective-permute-start(bf16[768,128]{1,0:T(8,128)(2,1)S(1)} %slice_bitcast_fusion), channel_id=1, source_target_pairs={{0,224},{8,232},{16,240},{24,248},{32,0},{40,8},{48,16},{56,24},{6... | collective-permute-start | bytes 589832 | tf_op jit(solution)/shard_map/ppermute | solution.py:553
  58.9 5.8 %collective-permute-start.13 = (bf16[768,128]{1,0:T(8,128)(2,1)S(1)}, bf16[768,128]{1,0:T(8,128)(2,1)S(1)}, u32[]{:S(2)}, u32[]{:S(2)}) collective-permute-start(bf16[768,128]{1,0:T(8,128)(2,1)S(1)} %slice_bitcast_fusion.1), channel_id=1, source_target_pairs={{0,32},{8,40},{16,48},{24,56},{32,64},{40,72},{48,80},{56,88},{64,... | collective-permute-start | bytes 589832 | tf_op jit(solution)/shard_map/ppermute | solution.py:553
  59.2 13.1 %collective-permute-start.19 = (bf16[256,768]{1,0:T(8,128)(2,1)S(1)}, bf16[256,768]{1,0:T(8,128)(2,1)S(1)}, u32[]{:S(2)}, u32[]{:S(2)}) collective-permute-start(bf16[256,768]{1,0:T(8,128)(2,1)S(1)} %get-tuple-element.92), channel_id=1, source_target_pairs={{0,4},{2,6},{4,0},{6,2},{1,5},{3,7},{5,1},{7,3},{8,12},{10,14},{12... | collective-permute-start | bytes 1179656 | tf_op jit(solution)/shard_map/ppermute | solution.py:550
  65.7 8.5 %collective-permute-start.16 = (bf16[2,144,384]{2,1,0:T(8,128)(2,1)S(1)}, bf16[2,144,384]{2,1,0:T(8,128)(2,1)S(1)}, u32[]{:S(2)}, u32[]{:S(2)}) collective-permute-start(bf16[2,144,384]{2,1,0:T(8,128)(2,1)S(1)} %get-tuple-element.81), channel_id=1, source_target_pairs={{0,16},{8,24},{16,0},{24,8},{32,48},{40,56},{48,32},{56,40},{64,80... | collective-permute-start | bytes 663560 | tf_op jit(solution)/shard_map/ppermute | solution.py:574
  70.8 6.4 %collective-permute-start.17 = (bf16[2,144,384]{2,1,0:T(8,128)(2,1)S(1)}, bf16[2,144,384]{2,1,0:T(8,128)(2,1)S(1)}, u32[]{:S(2)}, u32[]{:S(2)}) collective-permute-start(bf16[2,144,384]{2,1,0:T(8,128)(2,1)S(1)} %get-tuple-element.82), channel_id=1, source_target_pairs={{0,24},{8,0},{16,8},{24,16},{32,56},{40,32},{48,40},{56,48},{64,88... | collective-permute-start | bytes 663560 | tf_op jit(solution)/shard_map/ppermute | solution.py:574
  70.8 8.5 %collective-permute-start.18 = (bf16[2,144,384]{2,1,0:T(8,128)(2,1)S(1)}, bf16[2,144,384]{2,1,0:T(8,128)(2,1)S(1)}, u32[]{:S(2)}, u32[]{:S(2)}) collective-permute-start(bf16[2,144,384]{2,1,0:T(8,128)(2,1)S(1)} %get-tuple-element.83), channel_id=1, source_target_pairs={{0,8},{8,16},{16,24},{24,0},{32,40},{40,48},{48,56},{56,32},{64,72... | collective-permute-start | bytes 663560 | tf_op jit(solution)/shard_map/ppermute | solution.py:574
  79.6 5.8 %collective-permute-start.20 = (bf16[384,256]{1,0:T(8,128)(2,1)S(1)}, bf16[384,256]{1,0:T(8,128)(2,1)S(1)}, u32[]{:S(2)}, u32[]{:S(2)}) collective-permute-start(bf16[384,256]{1,0:T(8,128)(2,1)S(1)} %shard_map.109.refs_0_), channel_id=1, source_target_pairs={{0,2},{2,4},{4,6},{6,0},{1,3},{3,5},{5,7},{7,1},{8,10},{10,12},{12... | collective-permute-start | bytes 589832 | tf_op jit(solution)/shard_map/ppermute | solution.py:577
  79.7 8.8 %collective-permute-start.21 = (bf16[384,256]{1,0:T(8,128)(2,1)S(1)}, bf16[384,256]{1,0:T(8,128)(2,1)S(1)}, u32[]{:S(2)}, u32[]{:S(2)}) collective-permute-start(bf16[384,256]{1,0:T(8,128)(2,1)S(1)} %shard_map.109.refs_0_), channel_id=1, source_target_pairs={{0,4},{2,6},{4,0},{6,2},{1,5},{3,7},{5,1},{7,3},{8,12},{10,14},{12... | collective-permute-start | bytes 589832 | tf_op jit(solution)/shard_map/ppermute | solution.py:577
  83.2 5.3 %collective-permute-start.22 = (bf16[384,256]{1,0:T(8,128)(2,1)S(1)}, bf16[384,256]{1,0:T(8,128)(2,1)S(1)}, u32[]{:S(2)}, u32[]{:S(2)}) collective-permute-start(bf16[384,256]{1,0:T(8,128)(2,1)S(1)} %shard_map.109.refs_0_), channel_id=1, source_target_pairs={{0,6},{2,0},{4,2},{6,4},{1,7},{3,1},{5,3},{7,5},{8,14},{10,8},{12,... | collective-permute-start | bytes 589832 | tf_op jit(solution)/shard_map/ppermute | solution.py:577
  89.6 6.3 %collective-permute-start.23 = (bf16[384,384]{1,0:T(8,128)(2,1)S(1)}, bf16[384,384]{1,0:T(8,128)(2,1)S(1)}, u32[]{:S(2)}, u32[]{:S(2)}) collective-permute-start(bf16[384,384]{1,0:T(8,128)(2,1)S(1)} %shard_map.111), channel_id=1, source_target_pairs={{0,1},{1,0},{2,3},{3,2},{4,5},{5,4},{6,7},{7,6},{8,9},{9,8},{10,11... | collective-permute-start | bytes 884744 | tf_op jit(solution)/shard_map/ppermute | solution.py:579
  (8 other events, 40.9 us)

commit v3 on v2

--- a/solution.py
+++ b/solution.py
@@ -562,17 +562,16 @@
     right_2 = lax.optimization_barrier((state[0], right_2))[1]
     left_2 = lax.optimization_barrier((state[0], left_2))[1]
     right_3, left_3 = ring(right_2, left_2)
-    info, weights[1] = lax.optimization_barrier((info, weights[1]))
+    info, weights[2] = lax.optimization_barrier((info, weights[2]))
     state = attend(info, queries, spans, {2: (right_2,), SEQ_Z - 2: (left_2,)}, state)
     right_3 = lax.optimization_barrier((state[0], right_3))[1]
     left_3 = lax.optimization_barrier((state[0], left_3))[1]
     far = ring(right_3[0], left_3[1])
-    info, weights[3] = lax.optimization_barrier((info, weights[3]))
+    info, weights[1], weights[3] = lax.optimization_barrier((info, weights[1], weights[3]))
     state = attend(info, queries, spans, {3: (right_3,), SEQ_Z - 3: (left_3,)}, state)
     parts = attend(info, queries, spans, {half: far}, state, last=True)
 
     parts = [parts[0]] + [lax.ppermute(parts[g], "seq", around_y(-g)) for g in (2, 1, 3)]
-    *parts, weights[2] = lax.optimization_barrier((*parts, weights[2]))
     attended = merge(parts)
     rows = [attended] + [lax.ppermute(attended, "cache", around_x(s)) for s in (1, 2, 3)]
     theirs = output(where, rows, weights, True, jnp.bfloat16)

time: 97 us -> 97.4 us (level)
  waiting for transfers between devices: 23.7 us -> 21.2 us
  Pallas kernels: 22.3 us -> 24.6 us
    ppermute x3, starting transfers between devices: 3.6 us -> 7.65 us  [per_device(): lax.ppermute(attended, 'cache', around_x(s))]
    ppermute x3, starting transfers between devices: 6.57 us -> 4.03 us  [per_device(): lax.ppermute(parts[g], 'seq', around_y(-g))]
    pallas_call x5, Pallas kernels: 9.42 us -> 11.7 us  [attend(): pl.pallas_call(functools.partial(attend_kernel, first, last, tuple(blocks...]
    ppermute x4, starting transfers between devices: 13.9 us -> 11.7 us  [ring(): lax.ppermute(left, 'seq', around_z(-1))]
    ppermute x4, waiting for transfers between devices: 6.07 us -> 4.28 us  [ring(): lax.ppermute(left, 'seq', around_z(-1))]
    ppermute x4, starting transfers between devices: 0.28 us -> 1.69 us  [ring(): lax.ppermute(right, 'seq', around_z(1))]
    ppermute x3, waiting for transfers between devices: 6.99 us -> 5.93 us  [per_device(): lax.ppermute(parts[g], 'seq', around_y(-g))]
  transfers between devices with their start and end apart: 24 -> 24, of which waited for: 12 -> 12; matrix products, arithmetic and copies ran while one was open for 2% -> 2% of each run, Pallas kernels for 17% -> 18%
where the time goes in v3:
time: 97.4 us; the launch traced here: 96.7 us
  starting transfers between devices  43.7 us (45%)
  Pallas kernels  24.6 us (25%)
  waiting for transfers between devices  21.2 us (22%)
  local copies, waits for them, and re-layouts  4.59 us (5%)
  other arithmetic  2.34 us (2%)
    ppermute x4, starting transfers between devices, ring(): lax.ppermute(left, 'seq', around_z(-1))  11.7 us
    pallas_call x5, Pallas kernels, attend(): pl.pallas_call(functools.partial(attend_kernel, first, last, tuple(blocks...  11.7 us
    ppermute x3, starting transfers between devices, per_device(): lax.ppermute(attended, 'cache', around_x(s))  7.65 us
    ppermute x3, waiting for transfers between devices, per_device(): lax.ppermute(parts[g], 'seq', around_y(-g))  5.93 us
    ppermute x3, starting transfers between devices, per_device(): lax.ppermute(messages[s], 'cache', around_x(s))  5.72 us
    ppermute x4, waiting for transfers between devices, ring(): lax.ppermute(right, 'seq', around_z(1))  5.47 us
    ppermute x3, starting transfers between devices, per_device(): lax.ppermute(query, 'seq', around_y(s))  5.06 us
    ppermute x3, waiting for transfers between devices, per_device(): lax.ppermute(attended, 'cache', around_x(s))  4.97 us
  transfers between devices with their start and end apart: 24, of which 12 were waited for; matrix products, arithmetic and copies ran while one was open for 2% of the time, Pallas kernels for 18%

profile of v3, /device:TPU:1, one launch (start us, length us, event | category | flops | bytes accessed | tf_op | source)
XLA Modules:
  0.0 96.7 jit_solution(2170321580285360864)
XLA Ops:
  1.4 4.8 %shard_map.100 = (bf16[896,128]{1,0:T(8,128)(2,1)}, bf16[896,128]{1,0:T(8,128)(2,1)}, bf16[896,128]{1,0:T(8,128)(2,1)}, bf16[896,128]{1,0:T(8,128)(2,1)}, s32[2,8,768]{2,1,0:T(8,128)}, /*index=5*/s32[32]{0:T(128)}) custom-call(s32[43]{0:T(128)} %pad_add_fusion.1.where, bf16[384,3072]{1,0:T(8,128)(2,1)} %tokens.3, bf16[2,3072,128]{2,1,0:T(8,128)(2,1)} %down.1, ...), custom_call_target="tpu_custom_call" | custom-call | flops 600000000 | bytes 6291456 | tf_op jit(solution)/shard_map/pallas_call | solution.py:158
  6.3 2.1 %collective-permute-start = (bf16[896,128]{1,0:T(8,128)(2,1)}, bf16[896,128]{1,0:T(8,128)(2,1)S(1)}, u32[]{:S(2)}, u32[]{:S(2)}) collective-permute-start(bf16[896,128]{1,0:T(8,128)(2,1)} %get-tuple-element.54), channel_id=1, source_target_pairs={{0,2},{2,4},{4,6},{6,0},{1,3},{3,5},{5,7},{7,1},{8,10},{10,12},{12... | collective-permute-start | bytes 688136 | tf_op jit(solution)/shard_map/ppermute | solution.py:536
  8.4 2.5 %collective-permute-start.1 = (bf16[896,128]{1,0:T(8,128)(2,1)}, bf16[896,128]{1,0:T(8,128)(2,1)S(1)}, u32[]{:S(2)}, u32[]{:S(2)}) collective-permute-start(bf16[896,128]{1,0:T(8,128)(2,1)} %get-tuple-element.55), channel_id=1, source_target_pairs={{0,4},{2,6},{4,0},{6,2},{1,5},{3,7},{5,1},{7,3},{8,12},{10,14},{12... | collective-permute-start | bytes 688136 | tf_op jit(solution)/shard_map/ppermute | solution.py:536
  15.1 2.1 %shard_map.101 = (f32[384,256]{1,0:T(8,128)S(1)}, f32[384,256]{1,0:T(8,128)S(1)}) custom-call(bf16[384,3072]{1,0:T(8,128)(2,1)S(1)} %copy-done, bf16[3072,256]{1,0:T(8,128)(2,1)S(1)} %copy-done.1, bf16[3072,256]{1,0:T(8,128)(2,1)S(1)} %copy-done.2), custom_call_target="tpu_custom_call" | custom-call | flops 1200000000 | bytes 6291456 | tf_op jit(solution)/shard_map/pallas_call | solution.py:245
  20.1 2.6 %collective-permute-start.7 = (bf16[2,128,384]{2,1,0:T(8,128)(2,1)S(1)}, bf16[2,128,384]{2,1,0:T(8,128)(2,1)S(1)}, u32[]{:S(2)}, u32[]{:S(2)}) collective-permute-start(bf16[2,128,384]{2,1,0:T(8,128)(2,1)S(1)} %shard_map.103), channel_id=1, source_target_pairs={{0,16},{8,24},{16,0},{24,8},{32,48},{40,56},{48,32},{56,40},{64,80... | collective-permute-start | bytes 589832 | tf_op jit(solution)/shard_map/ppermute | solution.py:540
  23.9 1.8 %shard_map.102.refs_0_ = bf16[2,768,128]{2,1,0:T(8,128)(2,1)S(1)} custom-call(s32[43]{0:T(128)S(1)} %copy-done.6, f32[384,256]{1,0:T(8,128)S(1)} %get-tuple-element.51.key, f32[384,256]{1,0:T(8,128)S(1)} %get-tuple-element.52.value, bf16[896,128]{1,0:T(8,128)(2,1)S(1)} %copy-done.5, bf16[896,128]{1,0:T(8,128)(2,1)S(1)} %collective-permute-done.refs_1_, ...), custom_call_target="tpu_custom_call" | custom-call | flops 400000000 | bytes 2097152 | tf_op jit(solution)/shard_map/pallas_call | solution.py:288
  25.7 5.7 %collective-permute-start.10 = (bf16[2,768,128]{2,1,0:T(8,128)(2,1)S(1)}, bf16[2,768,128]{2,1,0:T(8,128)(2,1)}, u32[]{:S(2)}, u32[]{:S(2)}) collective-permute-start(bf16[2,768,128]{2,1,0:T(8,128)(2,1)S(1)} %shard_map.102.refs_0_), channel_id=1, source_target_pairs={{0,224},{8,232},{16,240},{24,248},{32,0},{40,8},{48,16},{56,24},{6... | collective-permute-start | bytes 1179656 | tf_op jit(solution)/shard_map/ppermute | solution.py:553
  31.6 3.6 %shard_map.104 = (f32[2,2,128,768]{3,2,1,0:T(8,128)S(1)}, f32[2,2,8,768]{3,2,1,0:T(8,128)S(1)}) custom-call(s32[32]{0:T(128)S(1)} %copy-done.7, bf16[2,2,128,768]{3,2,1,0:T(8,128)(2,1)S(1)} %pad_maximum_fusion.queries, s32[2,8,768]{2,1,0:T(8,128)S(1)} %copy-done.4, bf16[2,768,128]{2,1,0:T(8,128)(2,1)S(1)} %shard_map.102.refs_0_), custom_call_target="tpu_custom_call" | custom-call | flops 1000000 | bytes 1048576 | tf_op jit(solution)/shard_map/pallas_call | solution.py:433
  35.2 2.3 %collective-permute-done.10.refs_1_ = bf16[2,768,128]{2,1,0:T(8,128)(2,1)} collective-permute-done((bf16[2,768,128]{2,1,0:T(8,128)(2,1)S(1)}, bf16[2,768,128]{2,1,0:T(8,128)(2,1)}, u32[]{:S(2)}, u32[]{:S(2)}) %collective-permute-start.10) | collective-permute-done | bytes 393248 | tf_op jit(solution)/shard_map/ppermute | solution.py:553
  37.4 3.5 %collective-permute-start.12 = (bf16[2,768,128]{2,1,0:T(8,128)(2,1)}, bf16[2,768,128]{2,1,0:T(8,128)(2,1)S(1)}, u32[]{:S(2)}, u32[]{:S(2)}) collective-permute-start(bf16[2,768,128]{2,1,0:T(8,128)(2,1)} %collective-permute-done.10.refs_1_), channel_id=1, source_target_pairs={{0,224},{8,232},{16,240},{24,248},{32,0},{40,8},{48,16},{56,24},{6... | collective-permute-start | bytes 1179656 | tf_op jit(solution)/shard_map/ppermute | solution.py:553
  42.7 4.6 %shard_map.105 = (f32[2,2,128,768]{3,2,1,0:T(8,128)S(1)}, f32[2,2,8,768]{3,2,1,0:T(8,128)S(1)}) custom-call(s32[32]{0:T(128)S(1)} %copy-done.7, bf16[2,2,128,768]{3,2,1,0:T(8,128)(2,1)S(1)} %pad_maximum_fusion.queries, s32[2,8,768]{2,1,0:T(8,128)S(1)} %copy-done.4, bf16[2,768,128]{2,1,0:T(8,128)(2,1)S(1)} %collective-permute-done.9.refs_0_, ...), custom_call_target="tpu_custom_call" | custom-call | flops 2000000 | bytes 1048576 | tf_op jit(solution)/shard_map/pallas_call | solution.py:433
  47.3 2.4 %collective-permute-start.15 = (bf16[2,768,128]{2,1,0:T(8,128)(2,1)S(1)}, bf16[2,768,128]{2,1,0:T(8,128)(2,1)S(1)}, u32[]{:S(2)}, u32[]{:S(2)}) collective-permute-start(bf16[2,768,128]{2,1,0:T(8,128)(2,1)S(1)} %collective-permute-done.12.refs_1_), channel_id=1, source_target_pairs={{0,224},{8,232},{16,240},{24,248},{32,0},{40,8},{48,16},{56,24},{6... | collective-permute-start | bytes 1179656 | tf_op jit(solution)/shard_map/ppermute | solution.py:553
  50.0 2.4 %collective-permute-start.5 = (bf16[256,768]{1,0:T(8,128)(2,1)S(1)}, bf16[256,768]{1,0:T(8,128)(2,1)S(1)}, u32[]{:S(2)}, u32[]{:S(2)}) collective-permute-start(bf16[256,768]{1,0:T(8,128)(2,1)S(1)} %get-tuple-element.84), channel_id=1, source_target_pairs={{0,6},{2,0},{4,2},{6,4},{1,7},{3,1},{5,3},{7,5},{8,14},{10,8},{12,... | collective-permute-start | bytes 1179656 | tf_op jit(solution)/shard_map/ppermute | solution.py:550
  52.4 1.8 %shard_map.106 = (f32[2,2,128,768]{3,2,1,0:T(8,128)S(1)}, f32[2,2,8,768]{3,2,1,0:T(8,128)S(1)}) custom-call(s32[32]{0:T(128)S(1)} %copy-done.7, bf16[2,2,128,768]{3,2,1,0:T(8,128)(2,1)S(1)} %pad_maximum_fusion.queries, s32[2,8,768]{2,1,0:T(8,128)S(1)} %copy-done.4, bf16[2,768,128]{2,1,0:T(8,128)(2,1)} %collective-permute-done.11.refs_0_, ...), custom_call_target="tpu_custom_call" | custom-call | flops 2000000 | bytes 1048576 | tf_op jit(solution)/shard_map/pallas_call | solution.py:433
  54.4 3.3 %collective-permute-done.13.refs_0_ = bf16[2,768,128]{2,1,0:T(8,128)(2,1)S(1)} collective-permute-done((bf16[2,768,128]{2,1,0:T(8,128)(2,1)}, bf16[2,768,128]{2,1,0:T(8,128)(2,1)S(1)}, u32[]{:S(2)}, u32[]{:S(2)}) %collective-permute-start.13) | collective-permute-done | bytes 393248 | tf_op jit(solution)/shard_map/ppermute | solution.py:553
  58.0 1.7 %collective-permute-start.14 = (bf16[768,128]{1,0:T(8,128)(2,1)S(1)}, bf16[768,128]{1,0:T(8,128)(2,1)S(1)}, u32[]{:S(2)}, u32[]{:S(2)}) collective-permute-start(bf16[768,128]{1,0:T(8,128)(2,1)S(1)} %slice_bitcast_fusion.1), channel_id=1, source_target_pairs={{0,32},{8,40},{16,48},{24,56},{32,64},{40,72},{48,80},{56,88},{64,... | collective-permute-start | bytes 589832 | tf_op jit(solution)/shard_map/ppermute | solution.py:553
  60.9 1.8 %collective-permute-done.16.refs_1_ = bf16[768,128]{1,0:T(8,128)(2,1)S(1)} collective-permute-done((bf16[768,128]{1,0:T(8,128)(2,1)S(1)}, bf16[768,128]{1,0:T(8,128)(2,1)S(1)}, u32[]{:S(2)}, u32[]{:S(2)}) %collective-permute-start.16) | collective-permute-done | bytes 196640 | tf_op jit(solution)/shard_map/ppermute | solution.py:553
  62.7 2.1 %collective-permute-done.14.refs_0_ = bf16[768,128]{1,0:T(8,128)(2,1)S(1)} collective-permute-done((bf16[768,128]{1,0:T(8,128)(2,1)S(1)}, bf16[768,128]{1,0:T(8,128)(2,1)S(1)}, u32[]{:S(2)}, u32[]{:S(2)}) %collective-permute-start.14) | collective-permute-done | bytes 196640 | tf_op jit(solution)/shard_map/ppermute | solution.py:553
  65.8 2.6 %collective-permute-start.17 = (bf16[2,144,384]{2,1,0:T(8,128)(2,1)S(1)}, bf16[2,144,384]{2,1,0:T(8,128)(2,1)S(1)}, u32[]{:S(2)}, u32[]{:S(2)}) collective-permute-start(bf16[2,144,384]{2,1,0:T(8,128)(2,1)S(1)} %get-tuple-element.77), channel_id=1, source_target_pairs={{0,16},{8,24},{16,0},{24,8},{32,48},{40,56},{48,32},{56,40},{64,80... | collective-permute-start | bytes 663560 | tf_op jit(solution)/shard_map/ppermute | solution.py:574
  69.8 2.3 %collective-permute-done.17.refs_1_ = bf16[2,144,384]{2,1,0:T(8,128)(2,1)S(1)} collective-permute-done((bf16[2,144,384]{2,1,0:T(8,128)(2,1)S(1)}, bf16[2,144,384]{2,1,0:T(8,128)(2,1)S(1)}, u32[]{:S(2)}, u32[]{:S(2)}) %collective-permute-start.17) | collective-permute-done | bytes 221216 | tf_op jit(solution)/shard_map/ppermute | solution.py:574
  72.2 2.3 %collective-permute-done.18.refs_2_ = bf16[2,144,384]{2,1,0:T(8,128)(2,1)S(1)} collective-permute-done((bf16[2,144,384]{2,1,0:T(8,128)(2,1)S(1)}, bf16[2,144,384]{2,1,0:T(8,128)(2,1)S(1)}, u32[]{:S(2)}, u32[]{:S(2)}) %collective-permute-start.18) | collective-permute-done | bytes 221216 | tf_op jit(solution)/shard_map/ppermute | solution.py:574
  77.2 6.2 %collective-permute-start.21 = (bf16[384,256]{1,0:T(8,128)(2,1)S(1)}, bf16[384,256]{1,0:T(8,128)(2,1)S(1)}, u32[]{:S(2)}, u32[]{:S(2)}) collective-permute-start(bf16[384,256]{1,0:T(8,128)(2,1)S(1)} %shard_map.109.refs_0_), channel_id=1, source_target_pairs={{0,4},{2,6},{4,0},{6,2},{1,5},{3,7},{5,1},{7,3},{8,12},{10,14},{12... | collective-permute-start | bytes 589832 | tf_op jit(solution)/shard_map/ppermute | solution.py:576
  85.3 3.4 %collective-permute-done.21.refs_2_ = bf16[384,256]{1,0:T(8,128)(2,1)S(1)} collective-permute-done((bf16[384,256]{1,0:T(8,128)(2,1)S(1)}, bf16[384,256]{1,0:T(8,128)(2,1)S(1)}, u32[]{:S(2)}, u32[]{:S(2)}) %collective-permute-start.21) | collective-permute-done | bytes 196640 | tf_op jit(solution)/shard_map/ppermute | solution.py:576
  89.8 4.9 %collective-permute-start.23 = (bf16[384,384]{1,0:T(8,128)(2,1)S(1)}, bf16[384,384]{1,0:T(8,128)(2,1)S(1)}, u32[]{:S(2)}, u32[]{:S(2)}) collective-permute-start(bf16[384,384]{1,0:T(8,128)(2,1)S(1)} %shard_map.111), channel_id=1, source_target_pairs={{0,1},{1,0},{2,3},{3,2},{4,5},{5,4},{6,7},{7,6},{8,9},{9,8},{10,11... | collective-permute-start | bytes 884744 | tf_op jit(solution)/shard_map/ppermute | solution.py:578
  (61 shorter events, 23.8 us)
Async XLA Ops:
  6.3 16.5 %collective-permute-start = (bf16[896,128]{1,0:T(8,128)(2,1)}, bf16[896,128]{1,0:T(8,128)(2,1)S(1)}, u32[]{:S(2)}, u32[]{:S(2)}) collective-permute-start(bf16[896,128]{1,0:T(8,128)(2,1)} %get-tuple-element.54), channel_id=1, source_target_pairs={{0,2},{2,4},{4,6},{6,0},{1,3},{3,5},{5,7},{7,1},{8,10},{10,12},{12... | collective-permute-start | bytes 688136 | tf_op jit(solution)/shard_map/ppermute | solution.py:536
  8.4 15.5 %collective-permute-start.1 = (bf16[896,128]{1,0:T(8,128)(2,1)}, bf16[896,128]{1,0:T(8,128)(2,1)S(1)}, u32[]{:S(2)}, u32[]{:S(2)}) collective-permute-start(bf16[896,128]{1,0:T(8,128)(2,1)} %get-tuple-element.55), channel_id=1, source_target_pairs={{0,4},{2,6},{4,0},{6,2},{1,5},{3,7},{5,1},{7,3},{8,12},{10,14},{12... | collective-permute-start | bytes 688136 | tf_op jit(solution)/shard_map/ppermute | solution.py:536
  10.8 13.0 %collective-permute-start.2 = (bf16[896,128]{1,0:T(8,128)(2,1)}, bf16[896,128]{1,0:T(8,128)(2,1)S(1)}, u32[]{:S(2)}, u32[]{:S(2)}) collective-permute-start(bf16[896,128]{1,0:T(8,128)(2,1)} %get-tuple-element.56), channel_id=1, source_target_pairs={{0,6},{2,0},{4,2},{6,4},{1,7},{3,1},{5,3},{7,5},{8,14},{10,8},{12,... | collective-permute-start | bytes 688136 | tf_op jit(solution)/shard_map/ppermute | solution.py:536
  18.8 12.6 %collective-permute-start.6 = (bf16[2,128,384]{2,1,0:T(8,128)(2,1)S(1)}, bf16[2,128,384]{2,1,0:T(8,128)(2,1)S(1)}, u32[]{:S(2)}, u32[]{:S(2)}) collective-permute-start(bf16[2,128,384]{2,1,0:T(8,128)(2,1)S(1)} %shard_map.103), channel_id=1, source_target_pairs={{0,8},{8,16},{16,24},{24,0},{32,40},{40,48},{48,56},{56,32},{64,72... | collective-permute-start | bytes 589832 | tf_op jit(solution)/shard_map/ppermute | solution.py:540
  20.1 11.3 %collective-permute-start.7 = (bf16[2,128,384]{2,1,0:T(8,128)(2,1)S(1)}, bf16[2,128,384]{2,1,0:T(8,128)(2,1)S(1)}, u32[]{:S(2)}, u32[]{:S(2)}) collective-permute-start(bf16[2,128,384]{2,1,0:T(8,128)(2,1)S(1)} %shard_map.103), channel_id=1, source_target_pairs={{0,16},{8,24},{16,0},{24,8},{32,48},{40,56},{48,32},{56,40},{64,80... | collective-permute-start | bytes 589832 | tf_op jit(solution)/shard_map/ppermute | solution.py:540
  22.8 8.7 %collective-permute-start.8 = (bf16[2,128,384]{2,1,0:T(8,128)(2,1)S(1)}, bf16[2,128,384]{2,1,0:T(8,128)(2,1)S(1)}, u32[]{:S(2)}, u32[]{:S(2)}) collective-permute-start(bf16[2,128,384]{2,1,0:T(8,128)(2,1)S(1)} %shard_map.103), channel_id=1, source_target_pairs={{0,24},{8,0},{16,8},{24,16},{32,56},{40,32},{48,40},{56,48},{64,88... | collective-permute-start | bytes 589832 | tf_op jit(solution)/shard_map/ppermute | solution.py:540
  25.7 11.7 %collective-permute-start.10 = (bf16[2,768,128]{2,1,0:T(8,128)(2,1)S(1)}, bf16[2,768,128]{2,1,0:T(8,128)(2,1)}, u32[]{:S(2)}, u32[]{:S(2)}) collective-permute-start(bf16[2,768,128]{2,1,0:T(8,128)(2,1)S(1)} %shard_map.102.refs_0_), channel_id=1, source_target_pairs={{0,224},{8,232},{16,240},{24,248},{32,0},{40,8},{48,16},{56,24},{6... | collective-permute-start | bytes 1179656 | tf_op jit(solution)/shard_map/ppermute | solution.py:553
  31.4 9.6 %collective-permute-start.9 = (bf16[2,768,128]{2,1,0:T(8,128)(2,1)S(1)}, bf16[2,768,128]{2,1,0:T(8,128)(2,1)S(1)}, u32[]{:S(2)}, u32[]{:S(2)}) collective-permute-start(bf16[2,768,128]{2,1,0:T(8,128)(2,1)S(1)} %shard_map.102.refs_0_), channel_id=1, source_target_pairs={{0,32},{8,40},{16,48},{24,56},{32,64},{40,72},{48,80},{56,88},{64,... | collective-permute-start | bytes 1179656 | tf_op jit(solution)/shard_map/ppermute | solution.py:553
  37.4 9.9 %collective-permute-start.12 = (bf16[2,768,128]{2,1,0:T(8,128)(2,1)}, bf16[2,768,128]{2,1,0:T(8,128)(2,1)S(1)}, u32[]{:S(2)}, u32[]{:S(2)}) collective-permute-start(bf16[2,768,128]{2,1,0:T(8,128)(2,1)} %collective-permute-done.10.refs_1_), channel_id=1, source_target_pairs={{0,224},{8,232},{16,240},{24,248},{32,0},{40,8},{48,16},{56,24},{6... | collective-permute-start | bytes 1179656 | tf_op jit(solution)/shard_map/ppermute | solution.py:553
  41.0 8.7 %collective-permute-start.11 = (bf16[2,768,128]{2,1,0:T(8,128)(2,1)S(1)}, bf16[2,768,128]{2,1,0:T(8,128)(2,1)}, u32[]{:S(2)}, u32[]{:S(2)}) collective-permute-start(bf16[2,768,128]{2,1,0:T(8,128)(2,1)S(1)} %collective-permute-done.9.refs_0_), channel_id=1, source_target_pairs={{0,32},{8,40},{16,48},{24,56},{32,64},{40,72},{48,80},{56,88},{64,... | collective-permute-start | bytes 1179656 | tf_op jit(solution)/shard_map/ppermute | solution.py:553
  42.4 10.0 %collective-permute-start.3 = (bf16[256,768]{1,0:T(8,128)(2,1)S(1)}, bf16[256,768]{1,0:T(8,128)(2,1)S(1)}, u32[]{:S(2)}, u32[]{:S(2)}) collective-permute-start(bf16[256,768]{1,0:T(8,128)(2,1)S(1)} %get-tuple-element.86), channel_id=1, source_target_pairs={{0,4},{2,6},{4,0},{6,2},{1,5},{3,7},{5,1},{7,3},{8,12},{10,14},{12... | collective-permute-start | bytes 1179656 | tf_op jit(solution)/shard_map/ppermute | solution.py:550
  47.3 7.1 %collective-permute-start.15 = (bf16[2,768,128]{2,1,0:T(8,128)(2,1)S(1)}, bf16[2,768,128]{2,1,0:T(8,128)(2,1)S(1)}, u32[]{:S(2)}, u32[]{:S(2)}) collective-permute-start(bf16[2,768,128]{2,1,0:T(8,128)(2,1)S(1)} %collective-permute-done.12.refs_1_), channel_id=1, source_target_pairs={{0,224},{8,232},{16,240},{24,248},{32,0},{40,8},{48,16},{56,24},{6... | collective-permute-start | bytes 1179656 | tf_op jit(solution)/shard_map/ppermute | solution.py:553
  49.7 8.0 %collective-permute-start.13 = (bf16[2,768,128]{2,1,0:T(8,128)(2,1)}, bf16[2,768,128]{2,1,0:T(8,128)(2,1)S(1)}, u32[]{:S(2)}, u32[]{:S(2)}) collective-permute-start(bf16[2,768,128]{2,1,0:T(8,128)(2,1)} %collective-permute-done.11.refs_0_), channel_id=1, source_target_pairs={{0,32},{8,40},{16,48},{24,56},{32,64},{40,72},{48,80},{56,88},{64,... | collective-permute-start | bytes 1179656 | tf_op jit(solution)/shard_map/ppermute | solution.py:553
  49.7 10.4 %collective-permute-start.4 = (bf16[256,768]{1,0:T(8,128)(2,1)S(1)}, bf16[256,768]{1,0:T(8,128)(2,1)S(1)}, u32[]{:S(2)}, u32[]{:S(2)}) collective-permute-start(bf16[256,768]{1,0:T(8,128)(2,1)S(1)} %get-tuple-element.85), channel_id=1, source_target_pairs={{0,2},{2,4},{4,6},{6,0},{1,3},{3,5},{5,7},{7,1},{8,10},{10,12},{12... | collective-permute-start | bytes 1179656 | tf_op jit(solution)/shard_map/ppermute | solution.py:550
  50.0 10.1 %collective-permute-start.5 = (bf16[256,768]{1,0:T(8,128)(2,1)S(1)}, bf16[256,768]{1,0:T(8,128)(2,1)S(1)}, u32[]{:S(2)}, u32[]{:S(2)}) collective-permute-start(bf16[256,768]{1,0:T(8,128)(2,1)S(1)} %get-tuple-element.84), channel_id=1, source_target_pairs={{0,6},{2,0},{4,2},{6,4},{1,7},{3,1},{5,3},{7,5},{8,14},{10,8},{12,... | collective-permute-start | bytes 1179656 | tf_op jit(solution)/shard_map/ppermute | solution.py:550
  57.8 4.9 %collective-permute-start.16 = (bf16[768,128]{1,0:T(8,128)(2,1)S(1)}, bf16[768,128]{1,0:T(8,128)(2,1)S(1)}, u32[]{:S(2)}, u32[]{:S(2)}) collective-permute-start(bf16[768,128]{1,0:T(8,128)(2,1)S(1)} %slice_bitcast_fusion), channel_id=1, source_target_pairs={{0,224},{8,232},{16,240},{24,248},{32,0},{40,8},{48,16},{56,24},{6... | collective-permute-start | bytes 589832 | tf_op jit(solution)/shard_map/ppermute | solution.py:553
  58.0 6.9 %collective-permute-start.14 = (bf16[768,128]{1,0:T(8,128)(2,1)S(1)}, bf16[768,128]{1,0:T(8,128)(2,1)S(1)}, u32[]{:S(2)}, u32[]{:S(2)}) collective-permute-start(bf16[768,128]{1,0:T(8,128)(2,1)S(1)} %slice_bitcast_fusion.1), channel_id=1, source_target_pairs={{0,32},{8,40},{16,48},{24,56},{32,64},{40,72},{48,80},{56,88},{64,... | collective-permute-start | bytes 589832 | tf_op jit(solution)/shard_map/ppermute | solution.py:553
  65.8 6.4 %collective-permute-start.17 = (bf16[2,144,384]{2,1,0:T(8,128)(2,1)S(1)}, bf16[2,144,384]{2,1,0:T(8,128)(2,1)S(1)}, u32[]{:S(2)}, u32[]{:S(2)}) collective-permute-start(bf16[2,144,384]{2,1,0:T(8,128)(2,1)S(1)} %get-tuple-element.77), channel_id=1, source_target_pairs={{0,16},{8,24},{16,0},{24,8},{32,48},{40,56},{48,32},{56,40},{64,80... | collective-permute-start | bytes 663560 | tf_op jit(solution)/shard_map/ppermute | solution.py:574
  68.4 6.1 %collective-permute-start.18 = (bf16[2,144,384]{2,1,0:T(8,128)(2,1)S(1)}, bf16[2,144,384]{2,1,0:T(8,128)(2,1)S(1)}, u32[]{:S(2)}, u32[]{:S(2)}) collective-permute-start(bf16[2,144,384]{2,1,0:T(8,128)(2,1)S(1)} %get-tuple-element.78), channel_id=1, source_target_pairs={{0,24},{8,0},{16,8},{24,16},{32,56},{40,32},{48,40},{56,48},{64,88... | collective-permute-start | bytes 663560 | tf_op jit(solution)/shard_map/ppermute | solution.py:574
  69.8 6.0 %collective-permute-start.19 = (bf16[2,144,384]{2,1,0:T(8,128)(2,1)S(1)}, bf16[2,144,384]{2,1,0:T(8,128)(2,1)S(1)}, u32[]{:S(2)}, u32[]{:S(2)}) collective-permute-start(bf16[2,144,384]{2,1,0:T(8,128)(2,1)S(1)} %get-tuple-element.79), channel_id=1, source_target_pairs={{0,8},{8,16},{16,24},{24,0},{32,40},{40,48},{48,56},{56,32},{64,72... | collective-permute-start | bytes 663560 | tf_op jit(solution)/shard_map/ppermute | solution.py:574
  76.1 9.2 %collective-permute-start.20 = (bf16[384,256]{1,0:T(8,128)(2,1)S(1)}, bf16[384,256]{1,0:T(8,128)(2,1)S(1)}, u32[]{:S(2)}, u32[]{:S(2)}) collective-permute-start(bf16[384,256]{1,0:T(8,128)(2,1)S(1)} %shard_map.109.refs_0_), channel_id=1, source_target_pairs={{0,2},{2,4},{4,6},{6,0},{1,3},{3,5},{5,7},{7,1},{8,10},{10,12},{12... | collective-permute-start | bytes 589832 | tf_op jit(solution)/shard_map/ppermute | solution.py:576
  77.2 11.5 %collective-permute-start.21 = (bf16[384,256]{1,0:T(8,128)(2,1)S(1)}, bf16[384,256]{1,0:T(8,128)(2,1)S(1)}, u32[]{:S(2)}, u32[]{:S(2)}) collective-permute-start(bf16[384,256]{1,0:T(8,128)(2,1)S(1)} %shard_map.109.refs_0_), channel_id=1, source_target_pairs={{0,4},{2,6},{4,0},{6,2},{1,5},{3,7},{5,1},{7,3},{8,12},{10,14},{12... | collective-permute-start | bytes 589832 | tf_op jit(solution)/shard_map/ppermute | solution.py:576
  83.4 5.3 %collective-permute-start.22 = (bf16[384,256]{1,0:T(8,128)(2,1)S(1)}, bf16[384,256]{1,0:T(8,128)(2,1)S(1)}, u32[]{:S(2)}, u32[]{:S(2)}) collective-permute-start(bf16[384,256]{1,0:T(8,128)(2,1)S(1)} %shard_map.109.refs_0_), channel_id=1, source_target_pairs={{0,6},{2,0},{4,2},{6,4},{1,7},{3,1},{5,3},{7,5},{8,14},{10,8},{12,... | collective-permute-start | bytes 589832 | tf_op jit(solution)/shard_map/ppermute | solution.py:576
  89.8 6.1 %collective-permute-start.23 = (bf16[384,384]{1,0:T(8,128)(2,1)S(1)}, bf16[384,384]{1,0:T(8,128)(2,1)S(1)}, u32[]{:S(2)}, u32[]{:S(2)}) collective-permute-start(bf16[384,384]{1,0:T(8,128)(2,1)S(1)} %shard_map.111), channel_id=1, source_target_pairs={{0,1},{1,0},{2,3},{3,2},{4,5},{5,4},{6,7},{7,6},{8,9},{9,8},{10,11... | collective-permute-start | bytes 884744 | tf_op jit(solution)/shard_map/ppermute | solution.py:578
  (8 other events, 40.9 us)
